TPU v7x, 256 devices: a whole 4x4x8 slice. The times are simulated.
256 devices in a mesh: depth: 2 (over y_lo), freq: 128 (over z, x, y_hi, core).
Axes of the slice: x: 4, y: 4 (y_hi: 2, y_lo: 2; y = y_hi * 2 + y_lo), z: 8, core: 2. Of those that a mesh axis runs over, the one named last changes fastest.
Arguments:
- top_fields: bfloat16 [1, 256, 4, 256, 256], P(None, 'freq'), may hold values from -24 to 24
- slowness: float32 [2, 384, 384], P('depth'), may hold values from -5 to 5
- kernels: float32 [2, 256, 2, 81], P('depth', 'freq'), may hold values from -1 to 1
- offsets: int32 [1, 2], replicated, may hold values from 0 to 128
Outputs:
- image: float32 [2, 1, 8, 65536], P('depth', None, None, 'freq')
All inputs are finite; a program needn't handle non-finite values.
Results may differ from a plain program's by a relative error of at most 0.0029.
Values may be sent and summed in bfloat16 or wider, within the bound.
A program may use at most 192 MiB of HBM per device.

v0:
```python
import jax
import jax.numpy as jnp
from jax import lax
from jax.sharding import PartitionSpec as P

LAGS = 8


phase_gain = 3.0


def passed_along(block, axis, distance):
    devices = range(lax.axis_size(axis))
    route = [(i - distance, i) for i in devices if i - distance in devices]
    return lax.ppermute(block, axis, route)


def band_matrix(kernel_taps, size_y):
    freq_count = kernel_taps.shape[0]
    rows_in = jnp.arange(size_y, dtype=jnp.int32)[:, None]
    rows_out = jnp.arange(size_y, dtype=jnp.int32)[None, :]
    offset_grid = rows_in - rows_out + 4
    one_hot = (offset_grid[:, :, None] == jnp.arange(9, dtype=jnp.int32)[None, None, :]).astype(
        jnp.float32
    )
    taps_grid = kernel_taps.reshape(freq_count, 2, 9, 9)
    band = jnp.einsum("fcab,ijb->fcaij", taps_grid, one_hot, precision=lax.Precision.HIGHEST)
    band_real = band[:, 0]
    band_imag = band[:, 1]
    upper_rows = jnp.concatenate((band_real, band_imag), axis=-1)
    lower_rows = jnp.concatenate((-band_imag, band_real), axis=-1)
    blocks = jnp.stack((upper_rows, lower_rows), axis=2)
    return blocks.reshape(freq_count, 9 * 2 * size_y, 2 * size_y)


def convolve(wavefield, kernel_taps):
    shot_count = wavefield.shape[0]
    freq_count = wavefield.shape[1]
    size_x = wavefield.shape[3]
    size_y = wavefield.shape[4]
    matrix = band_matrix(kernel_taps, size_y)
    split_field = wavefield.reshape(shot_count, freq_count, 2, 2, size_x, size_y)
    padded = jnp.pad(split_field, ((0, 0), (0, 0), (0, 0), (0, 0), (4, 4), (0, 0)))
    pieces = [padded[:, :, :, :, shift_x : shift_x + size_x, :] for shift_x in range(9)]
    stacked = jnp.stack(pieces, axis=4)
    stacked = jnp.transpose(stacked, (0, 1, 2, 5, 4, 3, 6))
    stacked = stacked.reshape(shot_count, freq_count, 2, size_x, 9 * 2 * size_y)
    product = lax.dot_general(
        stacked,
        matrix,
        (((4,), (1,)), ((1,), (0,))),
        precision=lax.Precision.HIGHEST,
        preferred_element_type=jnp.float32,
    )
    product = jnp.moveaxis(product, 0, 1).reshape(shot_count, freq_count, 2, size_x, 2, size_y)
    return (product[:, :, :, :, 0, :], product[:, :, :, :, 1, :])


def extrapolate(wavefield, kernel_taps, screen_level, freq_weight):
    out_real, out_imag = convolve(wavefield, kernel_taps)
    angle_grid = (
        phase_gain * freq_weight[None, :, None, None, None] * screen_level[:, None, None, :, :]
    )
    cosine = jnp.cos(angle_grid)
    sine_grid = jnp.sin(angle_grid)
    new_real = out_real * cosine - out_imag * sine_grid
    new_imag = out_real * sine_grid + out_imag * cosine
    stacked = jnp.stack((new_real, new_imag), axis=3)
    return stacked.reshape(wavefield.shape)


def image_terms(wavefield, lag_count):
    half_lags = lag_count // 2
    size_x = wavefield.shape[3]
    padded = jnp.pad(wavefield, ((0, 0), (0, 0), (0, 0), (half_lags, half_lags), (0, 0)))
    collected = []
    for lag_index in range(lag_count):
        lag_shift = lag_index - half_lags
        source_part = padded[:, :, 0:2, half_lags - lag_shift : half_lags - lag_shift + size_x]
        receiver_part = padded[:, :, 2:4, half_lags + lag_shift : half_lags + lag_shift + size_x]
        collected.append(jnp.sum(source_part * receiver_part, axis=(1, 2)))
    return jnp.stack(collected, axis=1)


def screens_of(slowness, offsets, size_x, size_y):
    start_x = offsets[0, 0]
    start_y = offsets[0, 1]
    windows = [
        lax.dynamic_slice(
            slowness,
            (jnp.zeros((), jnp.int32), start_x, start_y),
            (slowness.shape[0], size_x, size_y),
        )
    ]
    return jnp.stack(windows, axis=1)


def freq_weights(first_freq, count_freqs, total_freqs):
    return (first_freq + jnp.arange(count_freqs, dtype=jnp.int32) + 1).astype(
        jnp.float32
    ) / total_freqs


def run_levels(start_field, kernel_batch, screens, weights, round_after):
    level_count = len(round_after)
    shot_count = start_field.shape[0]
    size_x = start_field.shape[3]
    size_y = start_field.shape[4]
    fields_first = jnp.moveaxis(start_field, 1, 0)
    kernels_first = jnp.moveaxis(kernel_batch, 1, 0)

    def one_freq(image_acc, items):
        field_one, kernel_one, weight_one = items
        wavefield = field_one[:, None].astype(jnp.float32)
        wavefield = extrapolate(wavefield, kernel_one[0][None], screens[0], weight_one[None])
        level_terms = [image_terms(wavefield, LAGS)]
        return (image_acc + jnp.stack(level_terms, axis=0), wavefield[:, 0])

    initial = jnp.zeros((level_count, shot_count, LAGS, size_x, size_y), jnp.float32)
    image_acc, finals = lax.scan(one_freq, initial, (fields_first, kernels_first, weights))
    return (jnp.moveaxis(finals, 0, 1), image_acc)


def local(top_fields, slowness, kernels, offsets):
    size_x = top_fields.shape[3]
    size_y = top_fields.shape[4]
    freq_local = top_fields.shape[1]
    depth_groups = lax.axis_size("depth")
    freq_groups = lax.axis_size("freq")
    total_freqs = freq_local * freq_groups
    slab_levels = slowness.shape[0]
    freq_start = lax.axis_index("freq") * freq_local
    depth_rank = lax.axis_index("depth")
    microbatches = 1
    batch_size = freq_local // microbatches
    screens = screens_of(slowness, offsets, size_x, size_y)
    round_after = [False]

    def run_section(section_index, incoming):
        micro_index = section_index - depth_rank
        clipped = jnp.clip(micro_index, 0, microbatches - 1)
        first_freq = clipped * batch_size
        start_field = jnp.where(depth_rank == 0, top_fields, incoming)
        weights = freq_weights(freq_start + first_freq, batch_size, total_freqs)
        wavefield, section_image = run_levels(start_field, kernels, screens, weights, round_after)
        in_range = jnp.logical_and(micro_index >= 0, micro_index < microbatches)
        contribution = jnp.where(in_range, section_image, 0.0)
        return (wavefield, contribution)

    def carry_step(section_index, state_pair):
        image_acc, incoming = state_pair
        wavefield, contribution = run_section(section_index, incoming)
        outgoing = passed_along(wavefield.astype(jnp.bfloat16), "depth", 1)
        return (image_acc + contribution, outgoing)

    section_count = microbatches + depth_groups - 1
    initial = (
        jnp.zeros((slab_levels, top_fields.shape[0], LAGS, size_x, size_y), jnp.float32),
        jnp.zeros((top_fields.shape[0], batch_size, 4, size_x, size_y), jnp.bfloat16),
    )
    image_acc, incoming = lax.fori_loop(0, section_count - 1, carry_step, initial)
    last_pair = run_section(section_count - 1, incoming)
    image_local = image_acc + last_pair[1]
    flat_image = image_local.reshape(image_local.shape[:3] + (size_x * size_y,))
    reduced = lax.psum_scatter(flat_image, "freq", scatter_dimension=3, tiled=True)
    return reduced * float(total_freqs) ** (-0.5)


def solution(mesh):
    placed = (
        P(None, "freq", None, None, None),
        P("depth", None, None),
        P("depth", "freq", None, None),
        P(),
    )
    return jax.shard_map(
        local, mesh=mesh, in_specs=placed, out_specs=P("depth", None, None, "freq"), check_vma=False
    )
```

profile of v0, /device:TPU:8, one launch (start us, length us, event | category | flops | bytes accessed | tf_op | source)
XLA Modules:
  0.0 1168.2 jit_solution(2882898711606156474)
XLA Ops:
  12.7 216.4 %while.38 = (s32[]{:T(128)}, f32[1,1,8,256,256]{4,3,2,1,0:T(8,128)}, bf16[2,1,4,256,256]{4,3,2,1,0:T(8,128)(2,1)}, bf16[2,1,4,256,256]{4,3,2,1,0:T(8,128)(2,1)S(...) while((s32[]{:T(128)}, ...), condition=%wide.region_9.10_spmd.clone, body=%wide.region_0.9_spmd.clone.sunk | while | flops 14632943616 | bytes 216010096 | solution.py:120
  16.9 4.2 slice_bitcast_fusion.10
  21.6 8.9 maximum_bitcast_fusion.6
  30.5 10.4 pad_maximum_fusion.8
  40.9 14.9 %copy.74 = f32[1,9,2,256,512]{4,3,2,1,0:T(8,128)} copy(f32[1,9,2,256,512]{4,1,3,2,0:T(8,128)} %pad_maximum_fusion.8) | data formatting | bytes 18874368 | tf_op jit(solution)/shard_map/while/body/eval_jaxpr/while/body/eval_jaxpr/stack | solution.py:32
  55.8 9.6 copy.75
  75.2 12.5 %reshape.466 = f32[2,256,4608,1]{2,1,0,3:T(8,128)} reshape(f32[1,1,2,256,9,2,256]{6,5,4,3,2,1,0:T(2,128)} %bitcast.377) | data formatting | bytes 18874368 | tf_op jit(solution)/shard_map/reshape.312
  87.7 18.6 %fusion.74 = f32[1,1,2,256,2,256]{5,3,4,2,1,0:T(8,128)S(1)} fusion(f32[2,256,4608,1]{2,1,0,3:T(8,128)} %bitcast.373, f32[2,256,4608,1]{2,1,0,3:T(8,128)} %reshape.466), kind=kOutput, calls=%fused_computation.13.clone.1 | convolution fusion | flops 14495514624 | bytes 19922944 | tf_op jit(solution)/shard_map/while/body/eval_jaxpr/while/body/eval_jaxpr/dot_general | solution.py:48
  124.8 4.2 slice_bitcast_fusion.10
  129.5 8.9 maximum_bitcast_fusion.6
  138.4 10.4 pad_maximum_fusion.8
  148.8 14.9 %copy.74 = f32[1,9,2,256,512]{4,3,2,1,0:T(8,128)} copy(f32[1,9,2,256,512]{4,1,3,2,0:T(8,128)} %pad_maximum_fusion.8) | data formatting | bytes 18874368 | tf_op jit(solution)/shard_map/while/body/eval_jaxpr/while/body/eval_jaxpr/stack | solution.py:32
  163.6 9.6 copy.75
  183.1 12.5 %reshape.466 = f32[2,256,4608,1]{2,1,0,3:T(8,128)} reshape(f32[1,1,2,256,9,2,256]{6,5,4,3,2,1,0:T(2,128)} %bitcast.377) | data formatting | bytes 18874368 | tf_op jit(solution)/shard_map/reshape.312
  195.6 18.6 %fusion.74 = f32[1,1,2,256,2,256]{5,3,4,2,1,0:T(8,128)S(1)} fusion(f32[2,256,4608,1]{2,1,0,3:T(8,128)} %bitcast.373, f32[2,256,4608,1]{2,1,0,3:T(8,128)} %reshape.466), kind=kOutput, calls=%fused_computation.13.clone.1 | convolution fusion | flops 14495514624 | bytes 19922944 | tf_op jit(solution)/shard_map/while/body/eval_jaxpr/while/body/eval_jaxpr/dot_general | solution.py:48
  231.7 25.5 %collective-permute-done = bf16[1,2,4,256,256]{4,3,2,1,0:T(8,128)(2,1)S(1)} collective-permute-done((bf16[1,2,4,256,256]{4,3,2,1,0:T(8,128)(2,1)S(1)}, bf16[1,2,4,256,256]{4,3,2,1,0:T(8,128)(2,1)S(1)}, u32[]{:S(2)}, u32[]{:S(2)}) %collective-permute-start) | collective-permute-done | bytes 1048608 | tf_op jit(solution)/shard_map/while/body/eval_jaxpr/ppermute | solution.py:15
  258.3 234.6 %while.39 = (s32[]{:T(128)}, f32[1,1,8,256,256]{4,3,2,1,0:T(8,128)}, bf16[2,1,4,256,256]{4,3,2,1,0:T(8,128)(2,1)}, f32[2,1,2,81]{3,2,1,0:T(2,128)S(1)}, f32[2]{0...) while((s32[]{:T(128)}, f32[1,1,8,256,256]{4,3,2,1,0:T(8,128)}, ...), condition=%wide.region_19.20_spmd.clone, body=%wide.region_10.19_spmd.clone.sunk | while | flops 14632943616 | bytes 230690192 | solution.py:120
  281.2 4.2 slice_bitcast_fusion.11
  285.9 8.9 maximum_bitcast_fusion.7
  294.7 10.4 pad_maximum_fusion.10
  305.1 14.9 %copy.79 = f32[1,9,2,256,512]{4,3,2,1,0:T(8,128)} copy(f32[1,9,2,256,512]{4,1,3,2,0:T(8,128)} %pad_maximum_fusion.10) | data formatting | bytes 18874368 | tf_op jit(solution)/shard_map/while/body/eval_jaxpr/stack | solution.py:32
  320.0 9.6 copy.80
  340.5 12.5 %reshape.468 = f32[2,256,4608,1]{2,1,0,3:T(8,128)} reshape(f32[1,1,2,256,9,2,256]{6,5,4,3,2,1,0:T(2,128)} %bitcast.378) | data formatting | bytes 18874368 | tf_op jit(solution)/shard_map/reshape.296
  353.0 18.6 %fusion.81 = f32[1,1,2,256,2,256]{5,3,4,2,1,0:T(8,128)S(1)} fusion(f32[2,256,4608,1]{2,1,0,3:T(8,128)} %bitcast.374, f32[2,256,4608,1]{2,1,0,3:T(8,128)} %reshape.468), kind=kOutput, calls=%fused_computation.81.clone.1 | convolution fusion | flops 14495514624 | bytes 19922944 | tf_op jit(solution)/shard_map/while/body/eval_jaxpr/dot_general | solution.py:48
  388.8 4.2 slice_bitcast_fusion.11
  393.5 8.9 maximum_bitcast_fusion.7
  402.4 10.4 pad_maximum_fusion.10
  412.8 14.9 %copy.79 = f32[1,9,2,256,512]{4,3,2,1,0:T(8,128)} copy(f32[1,9,2,256,512]{4,1,3,2,0:T(8,128)} %pad_maximum_fusion.10) | data formatting | bytes 18874368 | tf_op jit(solution)/shard_map/while/body/eval_jaxpr/stack | solution.py:32
  427.7 9.6 copy.80
  448.2 12.5 %reshape.468 = f32[2,256,4608,1]{2,1,0,3:T(8,128)} reshape(f32[1,1,2,256,9,2,256]{6,5,4,3,2,1,0:T(2,128)} %bitcast.378) | data formatting | bytes 18874368 | tf_op jit(solution)/shard_map/reshape.296
  460.6 18.6 %fusion.81 = f32[1,1,2,256,2,256]{5,3,4,2,1,0:T(8,128)S(1)} fusion(f32[2,256,4608,1]{2,1,0,3:T(8,128)} %bitcast.374, f32[2,256,4608,1]{2,1,0,3:T(8,128)} %reshape.468), kind=kOutput, calls=%fused_computation.81.clone.1 | convolution fusion | flops 14495514624 | bytes 19922944 | tf_op jit(solution)/shard_map/while/body/eval_jaxpr/dot_general | solution.py:48
  496.7 663.0 %reduce-scatter.2.cloned.1.call-done = f32[1,1,8,512]{3,2,1,0:T(8,128)} async-done(((f32[1,1,8,65536]{3,2,1,0:T(8,128)}), f32[1,1,8,512]{3,2,1,0:T(8,128)}) %reduce-scatter.2.cloned.1.call-update) | async-done | bytes 16400 | tf_op jit(solution)/shard_map/reduce_scatter | solution.py:165
  (164 shorter events, 123.2 us)
Async XLA Ops:
  6.5 5.3 copy-start
  6.5 1153.1 %reduce-scatter.2.cloned.1.call-start = ((), (), s32[]{:S(2)}) async-start(), calls=%async_computation.1 | async-start | bytes 2113536 | tf_op jit(solution)/shard_map/reduce_scatter | solution.py:165
  71.5 3.7 copy-start.2
  179.4 3.7 copy-start.2
  229.1 29.2 %copy-start.6 = (f32[2,1,2,81]{3,2,1,0:T(2,128)S(1)}, f32[2,1,2,81]{3,2,1,0:T(2,128)}, u32[]{:S(2)}) copy-start(f32[2,1,2,81]{3,2,1,0:T(2,128)} %get-tuple-element.527) | copy-start | bytes 3892
  230.4 26.8 %collective-permute-start = (bf16[1,2,4,256,256]{4,3,2,1,0:T(8,128)(2,1)S(1)}, bf16[1,2,4,256,256]{4,3,2,1,0:T(8,128)(2,1)S(1)}, u32[]{:S(2)}, u32[]{:S(2)}) collective-permute-start(bf16[1,2,4,256,256]{4,3,2,1,0:T(8,128)(2,1)S(1)} %fusion.50), channel_id=1, source_target_pairs={{0,128},{1,129},{2,130},{3,131},{4,132},{5,133},{6,134},{7,135},{8... | collective-permute-start | bytes 3145736 | tf_op jit(solution)/shard_map/while/body/eval_jaxpr/ppermute | solution.py:15
  336.8 3.7 copy-start.3
  375.1 6.6 copy-start.4
  384.0 1.3 copy-start.5
  444.4 3.7 copy-start.3
  482.8 6.6 copy-start.4
  491.6 1.3 copy-start.5
  492.9 668.1 %copy-start.1 = (f32[1,384,384]{2,1,0:T(8,128)S(1)}, f32[1,384,384]{2,1,0:T(8,128)}, u32[]{:S(2)}) copy-start(f32[1,384,384]{2,1,0:T(8,128)} %param.9) | copy-start | bytes 1769476
Sparse Core Ops, SparseCore 0:
  496.8 662.8 reduce-scatter.1
where the time goes:
time: 1190 us; the launch traced here: 1170 us
  waiting for transfers between devices  688 us (58%)
  local copies, waits for them, and re-layouts  241 us (20%)
  other arithmetic  109 us (9%)
  matrix products  88.3 us (7%)
  loops' own time  22.8 us (2%)
  between operations  17.6 us (1%)
    reduce_scatter x1, waiting for transfers between devices, local(): lax.psum_scatter(flat_image, 'freq', scatter_dimension=3, tiled=True)  663 us
    another operation x8, other arithmetic, band_matrix(): blocks = jnp.stack((upper_rows, lower_rows), axis=2)  77.1 us
    dot_general x4, matrix products, convolve(): lax.dot_general(stacked, matrix, (((4,), (1,)), ((1,), (0,))), precision=...  74.5 us
    another operation x4, local copies, waits for them, and re-layouts, band_matrix(): blocks = jnp.stack((upper_rows, lower_rows), axis=2)  59.4 us
    while x76, local copies, waits for them, and re-layouts  56.1 us
    another operation x8, local copies, waits for them, and re-layouts  50.2 us
    dot_general x4, local copies, waits for them, and re-layouts, convolve(): lax.dot_general(stacked, matrix, (((4,), (1,)), ((1,), (0,))), precision=...  38.5 us
    ppermute x1, waiting for transfers between devices, passed_along(): return lax.ppermute(block, axis, route)  25.5 us
  transfers between devices with their start and end apart: 2, of which 2 were waited for; matrix products, arithmetic and copies ran while one was open for 0% of the time, Pallas kernels for 0%

commit v1 on v0

v1 whole, which is shorter than its diff:
```python
import functools

import jax
import jax.numpy as jnp
from jax import lax
from jax.experimental import pallas as pl
from jax.experimental.pallas import tpu as pltpu
from jax.sharding import PartitionSpec as P

F32, BF16 = jnp.float32, jnp.bfloat16
MESH = pl.DeviceIdType.MESH

NZ, NXX = 8, 4


def iota(shape, dim):
    return lax.broadcasted_iota(jnp.int32, shape, dim)


def split_store(w_ref, rows, cols, value):
    high = value.astype(BF16)
    w_ref[0, rows, cols] = high
    w_ref[1, rows, cols] = (value - high.astype(F32)).astype(BF16)


def build_weights(taps_ref, w_ref, edge_ref):
    row, col = iota((128, 128), 0), iota((128, 128), 1)
    near = jnp.abs(col - row) <= 4
    row8, col8 = iota((8, 128), 0), iota((8, 128), 1)
    low = row8 < 4
    top_mask = col8 - row8 >= 124
    end_mask = col8 - (row8 + 120) <= -124
    edge_ref[...] = jnp.zeros_like(edge_ref)
    for a in range(9):
        circ = []
        for part in range(2):
            first = jnp.broadcast_to(taps_ref[part, a : a + 1, :], (128, 128))
            circ.append(pltpu.roll(first, 0, 1, stride=1, stride_axis=0))
        d_r, d_i = (jnp.where(near, m, 0.0) for m in circ)
        base = a * 256
        split_store(w_ref, pl.ds(base, 128), pl.ds(0, 128), d_r)
        split_store(w_ref, pl.ds(base, 128), pl.ds(128, 128), d_i)
        split_store(w_ref, pl.ds(base + 128, 128), pl.ds(0, 128), -d_i)
        split_store(w_ref, pl.ds(base + 128, 128), pl.ds(128, 128), d_r)
        t_r, t_i = (jnp.where(top_mask, m[0:8], 0.0) for m in circ)
        e_r, e_i = (jnp.where(end_mask, m[120:128], 0.0) for m in circ)
        rows = pl.ds(a * 8, 8)
        edge_ref[0, rows, 0:128] = jnp.where(low, t_r, -pltpu.roll(t_i, 4, 0))
        edge_ref[0, rows, 128:256] = jnp.where(low, t_i, pltpu.roll(t_r, 4, 0))
        edge_ref[1, rows, 0:128] = jnp.where(low, pltpu.roll(e_r, 4, 0), -e_i)
        edge_ref[1, rows, 128:256] = jnp.where(low, pltpu.roll(e_i, 4, 0), e_r)
    for side in range(2):
        split_store(w_ref, pl.ds(2304 + 128 * side, 128), pl.ds(0, 256), edge_ref[side])


def build_lhs(f_ref, g_ref, l_ref):
    lane = iota((264, 128), 1)
    for s in range(2):
        g_ref[s] = jnp.where(
            lane < 4, f_ref[2 + s, 0], jnp.where(lane < 8, pltpu.roll(f_ref[2 + s, 1], 4, 1), 0.0)
        )
        g_ref[2 + s] = jnp.where(
            lane < 4,
            pltpu.roll(f_ref[s, 0], 4, 1),
            jnp.where(lane < 8, pltpu.roll(f_ref[s, 1], 8, 1), 0.0),
        )
    for grp in range(4):

        @pl.loop(0, 8)
        def _(blk):
            row0 = pl.multiple_of(blk * 32, 32)
            out_rows = pl.ds(pl.multiple_of(grp * 256 + blk * 32, 32), 32)
            edge = jnp.zeros((32, 128), F32)
            for a in range(9):
                for part in range(2):
                    l_ref[out_rows, pl.ds(a * 256 + part * 128, 128)] = f_ref[
                        grp, part, pl.ds(row0 + a, 32), :
                    ].astype(BF16)
                piece = g_ref[grp, pl.ds(row0 + a, 32), :]
                edge = edge + (pltpu.roll(piece, 8 * a, 1) if a else piece)
            here = 2304 + 128 * (grp // 2)
            there = 2304 + 128 * (1 - grp // 2)
            l_ref[out_rows, pl.ds(here, 128)] = edge.astype(BF16)
            l_ref[out_rows, pl.ds(there, 128)] = jnp.zeros((32, 128), BF16)


def convolve(l_ref, w_ref, o_ref):
    @pl.loop(0, 2)
    def _(m):
        rows = pl.ds(pl.multiple_of(m * 512, 512), 512)
        left = l_ref[rows, :]
        o_ref[rows, :] = jnp.dot(left, w_ref[0], preferred_element_type=F32) + jnp.dot(
            left, w_ref[1], preferred_element_type=F32
        )


def apply_phase(o_ref, screen_ref, weight, f_ref):
    for yb in range(2):

        @pl.loop(0, 16)
        def _(blk):
            row0 = pl.multiple_of(blk * 16, 16)
            angle = (3.0 * weight) * screen_ref[pl.ds(row0, 16), pl.ds(yb * 128, 128)]
            cosine, sine = jnp.cos(angle), jnp.sin(angle)
            for s in range(2):
                grp = yb * 2 + s
                rows = pl.ds(pl.multiple_of(grp * 256 + row0, 16), 16)
                re = o_ref[rows, 0:128]
                im = o_ref[rows, 128:256]
                f_ref[grp, 0, pl.ds(row0 + 4, 16), :] = re * cosine - im * sine
                f_ref[grp, 1, pl.ds(row0 + 4, 16), :] = re * sine + im * cosine


def flip_source(f_ref, rev_ref):
    index = 7 - iota((8, 128), 0)
    for yb in range(2):
        for part in range(2):
            for t in range(33):
                rev_ref[yb, part, 8 * (32 - t) : 8 * (32 - t) + 8, :] = jnp.take_along_axis(
                    f_ref[yb * 2, part, 8 * t : 8 * t + 8, :], index, axis=0
                )


def image_piece(f_ref, rev_ref, img_ref, xx):
    for yb in range(2):

        @pl.loop(0, NZ)
        def _(z):
            blk = z * NXX + xx
            row0 = pl.multiple_of(blk * 8, 8)
            rev0 = pl.multiple_of(248 - blk * 8, 8)
            for j in range(8):
                s_rows = pl.ds(rev0 + (7 - j), 8)
                r_rows = pl.ds(row0 + j, 8)
                value = (
                    rev_ref[yb, 0, s_rows, :] * f_ref[yb * 2 + 1, 0, r_rows, :]
                    + rev_ref[yb, 1, s_rows, :] * f_ref[yb * 2 + 1, 1, r_rows, :]
                )
                to = pl.multiple_of(z * 64 + (j // 4) * 32 + (j % 2) * 16 + yb * 8, 8)
                img_ref[(j // 2) % 2, xx, pl.ds(to, 8), :] = value


def kernel(
    total,
    taps_ref, screen_ref, top_ref, out_ref,
    f_ref, g_ref, l_ref, w_ref, edge_ref, o_ref, rev_ref,
    taps_all, screens, img, rx1, tx2, rx2, acc2, rx3, acc3, rx4,
    local_sem, s0_send, s0_recv, s1_send, s1_recv, s2_send, s2_recv,
    s3_send, s3_recv, s4_send, s4_recv,
):
    d = lax.axis_index("depth")
    f = lax.axis_index("freq")
    core, yhi, xx, z = f % 2, (f // 2) % 2, (f // 4) % NXX, f // 16

    def device(depth=d, zc=z, xc=xx, yc=yhi, cc=core):
        return (depth, ((zc * NXX + xc) * 2 + yc) * 2 + cc)

    x_peers = [device(xc=(xx + off) % NXX) for off in range(1, NXX)]
    z_peers = [device(zc=(z + off) % NZ) for off in range(1, NZ)]
    core_peer = device(cc=1 - core)
    depth_peer = device(depth=1 - d)
    y_peers = [depth_peer, device(yc=1 - yhi), device(depth=1 - d, yc=1 - yhi)]
    everyone = [core_peer] + y_peers + x_peers + z_peers
    barrier = pltpu.get_barrier_semaphore()
    for peer in everyone:
        pl.semaphore_signal(barrier, inc=1, device_id=peer, device_id_type=MESH)

    own = [
        pltpu.make_async_copy(taps_ref.at[d], taps_all.at[d], local_sem.at[0]),
        pltpu.make_async_copy(screen_ref, screens.at[d], local_sem.at[1]),
    ]
    for copy in own:
        copy.start()

    f_ref[:, :, 0:8, :] = jnp.zeros((4, 2, 8, 128), F32)
    f_ref[:, :, 256:264, :] = jnp.zeros((4, 2, 8, 128), F32)
    for s in range(2):
        for part in range(2):
            for yb in range(2):
                f_ref[yb * 2 + s, part, 4:260, :] = top_ref[
                    d, 2 * s + part, :, yb * 128 : yb * 128 + 128
                ].astype(F32)

    pl.semaphore_wait(barrier, len(everyone))

    def remote(src, dst, send, recv, peer):
        return pltpu.make_async_remote_copy(
            src_ref=src, dst_ref=dst, send_sem=send, recv_sem=recv,
            device_id=peer, device_id_type=MESH,
        )

    swap_taps = remote(taps_ref.at[1 - d], taps_all.at[d], s0_send.at[0], s0_recv.at[0], depth_peer)
    swap_screen = remote(screen_ref, screens.at[d], s0_send.at[1], s0_recv.at[1], depth_peer)
    swap_taps.start()
    swap_screen.start()
    weight = (2 * f + d + 1).astype(F32) / total

    def stage1_copy(k, off):
        xp = (xx + off) % NXX
        return remote(
            img.at[k, 1 - core, xp], rx1.at[k, off], s1_send.at[k, off], s1_recv.at[k, off], core_peer
        )

    def stage2_copy(k, off):
        return remote(
            tx2.at[k, off - 1], rx2.at[k, off - 1],
            s2_send.at[k, off - 1], s2_recv.at[k, off - 1], x_peers[off - 1],
        )

    def stage3_copy(k, off):
        zp = (z + off) % NZ
        return remote(
            acc2.at[k, zp], rx3.at[k, off - 1],
            s3_send.at[k, off - 1], s3_recv.at[k, off - 1], z_peers[off - 1],
        )

    def stage4_keep(k):
        return remote(
            acc3.at[k, 1 - yhi], rx4.at[k, 0], s4_send.at[k, 0], s4_recv.at[k, 0], y_peers[1]
        )

    def stage4_give(k, yc):
        return remote(
            acc3.at[k, yc], rx4.at[k, 1 + yhi], s4_send.at[k, 1 + yc], s4_recv.at[k, 1 + yhi],
            device(depth=k, yc=yc),
        )

    def stage4_get(k, yc):
        return remote(
            acc3.at[k, 0], rx4.at[k, 1 + yc], s4_send.at[k, 0], s4_recv.at[k, 1 + yc], depth_peer
        )

    def make_image(k):
        flip_source(f_ref, rev_ref)
        for off in (1, 2, 3, 0):
            image_piece(f_ref, rev_ref, img.at[k], (xx + off) % NXX)
            stage1_copy(k, off).start()

    def after_core(k):
        for off in (1, 2, 3, 0):
            xp = (xx + off) % NXX
            stage1_copy(k, off).wait_recv()

            @pl.loop(0, 8)
            def _(part):
                rows = pl.ds(pl.multiple_of(part * 64, 64), 64)
                value = img[k, core, xp, rows, :] + rx1[k, off, rows, :]
                if off:
                    tx2[k, off - 1, rows, :] = value.astype(BF16)
                else:
                    acc2[k, part] = value

            if off:
                stage2_copy(k, off).start()

    def after_x(k):
        for off in range(1, NXX):
            stage2_copy(k, off).wait_recv()

        @pl.loop(0, NZ)
        def _(part):
            rows = pl.ds(pl.multiple_of(part * 64, 64), 64)
            value = acc2[k, part]
            for off in range(1, NXX):
                value = value + rx2[k, off - 1, rows, :].astype(F32)
            acc2[k, part] = value

        for off in range(1, NZ):
            stage3_copy(k, off).start()

    def after_z(k):
        for off in range(1, NZ):
            stage3_copy(k, off).wait_recv()
        value = acc2[k, z]
        for off in range(1, NZ):
            value = value + rx3[k, off - 1]
        acc3[k] = value.reshape(2, 32, 128)

        @pl.when(d == k)
        def _():
            stage4_keep(k).start()

        @pl.when(d != k)
        def _():
            for yc in range(2):
                stage4_give(k, yc).start()

    def after_y(k):
        @pl.when(d == k)
        def _():
            stage4_keep(k).wait_recv()
            for yc in range(2):
                stage4_get(k, yc).wait_recv()
            value = acc3[k, yhi] + rx4[k, 0] + rx4[k, 1] + rx4[k, 2]
            value = value * (total ** -0.5)
            for part in range(4):
                out_ref[:, part * 128 : part * 128 + 128] = value[part * 8 : part * 8 + 8]

    build_lhs(f_ref, g_ref, l_ref)
    own[0].wait()
    swap_taps.wait_recv()
    build_weights(taps_all.at[0], w_ref, edge_ref)
    convolve(l_ref, w_ref, o_ref)
    own[1].wait()
    swap_screen.wait_recv()
    apply_phase(o_ref, screens.at[0], weight, f_ref)
    make_image(0)
    build_lhs(f_ref, g_ref, l_ref)
    after_core(0)
    build_weights(taps_all.at[1], w_ref, edge_ref)
    convolve(l_ref, w_ref, o_ref)
    after_x(0)
    apply_phase(o_ref, screens.at[1], weight, f_ref)
    after_z(0)
    make_image(1)
    after_y(0)
    after_core(1)
    after_x(1)
    after_z(1)
    after_y(1)

    swap_taps.wait_send()
    swap_screen.wait_send()
    for k in range(2):
        for off in range(NXX):
            stage1_copy(k, off).wait_send()
        for off in range(1, NXX):
            stage2_copy(k, off).wait_send()
        for off in range(1, NZ):
            stage3_copy(k, off).wait_send()

        @pl.when(d == k)
        def _():
            stage4_keep(k).wait_send()

        @pl.when(d != k)
        def _():
            for yc in range(2):
                stage4_give(k, yc).wait_send()


def migrate(total, taps, screen, top):
    dma = pltpu.SemaphoreType.DMA
    vmem = pl.BlockSpec(memory_space=pltpu.VMEM)
    return pl.pallas_call(
        functools.partial(kernel, total),
        out_shape=jax.ShapeDtypeStruct((8, 512), F32),
        in_specs=[vmem] * 3,
        out_specs=vmem,
        scratch_shapes=[
            pltpu.VMEM((4, 2, 264, 128), F32),
            pltpu.VMEM((4, 264, 128), F32),
            pltpu.VMEM((1024, 2560), BF16),
            pltpu.VMEM((2, 2560, 256), BF16),
            pltpu.VMEM((2, 128, 256), F32),
            pltpu.VMEM((1024, 256), F32),
            pltpu.VMEM((2, 2, 264, 128), F32),
            pltpu.VMEM((2, 2, 16, 128), F32),
            pltpu.VMEM((2, 256, 256), F32),
            pltpu.VMEM((2, 2, NXX, 512, 128), F32),
            pltpu.VMEM((2, NXX, 512, 128), F32),
            pltpu.VMEM((2, 3, 512, 128), BF16),
            pltpu.VMEM((2, 3, 512, 128), BF16),
            pltpu.VMEM((2, NZ, 64, 128), F32),
            pltpu.VMEM((2, 7, 64, 128), F32),
            pltpu.VMEM((2, 2, 32, 128), F32),
            pltpu.VMEM((2, 3, 32, 128), F32),
            dma((2,)), dma((2,)), dma((2,)), dma((2, 4)), dma((2, 4)), dma((2, 3)), dma((2, 3)),
            dma((2, 7)), dma((2, 7)), dma((2, 3)), dma((2, 3)),
        ],
        compiler_params=pltpu.CompilerParams(
            collective_id=0, has_side_effects=True, vmem_limit_bytes=56 * 2**20
        ),
    )(taps, screen, top)


def arranged(kernels):
    taps = kernels.reshape(-1, 2, 9, 9)
    gap = jnp.zeros(taps.shape[:3] + (119,), F32)
    rows = jnp.concatenate((taps[..., 4::-1], gap, taps[..., :4:-1]), axis=-1)
    return jnp.pad(rows, ((0, 0), (0, 0), (0, 7), (0, 0)))


def local(total, top_fields, slowness, kernels, offsets):
    screen = lax.dynamic_slice(slowness[0], (offsets[0, 0], offsets[0, 1]), (256, 256))
    out = migrate(float(total), arranged(kernels[0]), screen, top_fields[0])
    return out[None, None]


def solution(mesh):
    return jax.shard_map(
        functools.partial(local, 256),
        mesh=mesh,
        in_specs=(
            P(None, "freq", None, None, None),
            P("depth", None, None),
            P("depth", "freq", None, None),
            P(),
        ),
        out_specs=P("depth", None, None, "freq"),
        check_vma=False,
    )
```

time: 1190 us -> 71.6 us (0.06); the launches traced: 1170 us -> 71.3 us
  waiting for transfers between devices: 688 us -> 0 us
  local copies, waits for them, and re-layouts: 241 us -> 4.39 us
  other arithmetic: 109 us -> 0.09 us
  matrix products: 88.3 us -> 0 us
  Pallas kernels: 0 us -> 63 us
  loops' own time: 22.8 us -> 0 us
  between operations: 17.6 us -> 3.82 us
    reduce_scatter x1 -> x0, waiting for transfers between devices: 663 us -> none  [local(): lax.psum_scatter(flat_image, 'freq', scatter_dimension=3, tiled=True)]
    another operation x24 -> x1, local copies, waits for them, and re-layouts: 115 us -> 0.08 us  [arranged(): taps = kernels.reshape(-1, 2, 9, 9)]
    dot_general x8 -> x0, matrix products: 88.3 us -> none  [the longest x4 74.5 us: convolve(): lax.dot_general(stacked, matrix, (((4,), (1,)), ((1,), (0,))), precision=...]
    another operation x13 -> x0, other arithmetic: 77.4 us -> none  [the longest x8 77.1 us: band_matrix(): blocks = jnp.stack((upper_rows, lower_rows), axis=2)]
    pallas_call x0 -> x1, Pallas kernels: none -> 63 us  [migrate(): pl.pallas_call(functools.partial(kernel, total), out_shape=jax.ShapeDtype...]
    while x76 -> x0, local copies, waits for them, and re-layouts: 56.1 us -> none
    dot_general x4 -> x0, local copies, waits for them, and re-layouts: 38.5 us -> none  [convolve(): lax.dot_general(stacked, matrix, (((4,), (1,)), ((1,), (0,))), precision=...]
    ppermute x1 -> x0, waiting for transfers between devices: 25.5 us -> none  [passed_along(): return lax.ppermute(block, axis, route)]
  transfers between devices with their start and end apart: 2 -> 0, of which waited for: 2 -> 0; matrix products, arithmetic and copies ran while one was open for 0% -> 0% of each run, Pallas kernels for 0% -> 0%
where the time goes in v1:
time: 71.6 us; the launch traced here: 71.3 us
  Pallas kernels  63 us (88%)
  local copies, waits for them, and re-layouts  4.39 us (6%)
  between operations  3.82 us (5%)
    pallas_call x1, Pallas kernels, migrate(): pl.pallas_call(functools.partial(kernel, total), out_shape=jax.ShapeDtype...  63 us
    unnamed x7, local copies, waits for them, and re-layouts  1.97 us

profile of v1, /device:TPU:8, one launch (start us, length us, event | category | flops | bytes accessed | tf_op | source)
XLA Modules:
  0.0 71.3 jit_solution(11071213476136716083)
XLA Ops:
  0.0 0.0 copy-start
  0.0 0.0 copy-start.2
  0.0 0.1 pad.6.clone
  0.1 0.6 copy-done.2
  0.7 0.6 fusion
  3.8 0.0 copy-start.1
  5.1 0.0 copy-done.1
  5.1 0.1 reshape_squeeze.3
  5.2 0.1 rev.6
  5.3 0.1 slice.17
  5.3 0.1 rev.7
  5.4 0.1 pad_maximum_fusion
  5.5 0.6 pad.4.taps_ref
  6.1 0.0 copy-done
  6.1 0.8 %dynamic-slice_bitcast_fusion.screen_ref = f32[256,256]{1,0:T(8,128)} fusion(f32[1,384,384]{2,1,0:T(8,128)S(1)} %copy-done, s32[]{:T(128)S(6)} %select_n.6, s32[]{:T(128)S(6)} %select_n.7), kind=kLoop, calls=%fused_computation | loop fusion | bytes 524296 | tf_op jit(solution)/shard_map/dynamic_slice | solution.py:385
  7.0 63.0 %shard_map.46 = f32[8,512]{1,0:T(8,128)} custom-call(f32[2,2,16,128]{3,2,1,0:T(8,128)} %pad.4.taps_ref, f32[256,256]{1,0:T(8,128)} %dynamic-slice_bitcast_fusion.screen_ref, bf16[2,4,256,256]{3,2,1,0:T(8,128)(2,1)} %bitcast.7), custom_call_target="tpu_custom_call" | custom-call | tf_op jit(solution)/shard_map/pallas_call | solution.py:345
  70.0 1.3 %copy.6 = f32[1,1,8,512]{3,2,1,0:T(8,128)} copy(f32[1,1,8,512]{3,2,1,0:T(8,128)} %bitcast.9) | data formatting | bytes 32768
  (1 shorter events, 0.0 us)
Async XLA Ops:
  0.0 6.1 %copy-start = (f32[1,384,384]{2,1,0:T(8,128)S(1)}, f32[1,384,384]{2,1,0:T(8,128)}, u32[]{:S(2)}) copy-start(f32[1,384,384]{2,1,0:T(8,128)} %param.5) | copy-start | bytes 1769476
  0.0 0.7 %copy-start.2 = (s32[1,2]{1,0:T(1,128)S(1)}, s32[1,2]{1,0:T(1,128)}, u32[]{:S(2)}) copy-start(s32[1,2]{1,0:T(1,128)} %param.7) | copy-start | bytes 28
  3.8 1.3 %copy-start.1 = (f32[1,2,2,81]{3,2,1,0:T(2,128)S(1)}, f32[1,2,2,81]{3,2,1,0:T(2,128)}, u32[]{:S(2)}) copy-start(f32[1,2,2,81]{3,2,1,0:T(2,128)} %param.6) | copy-start | bytes 3892

commit v2 on v1

v2 whole, which is shorter than its diff:
```python
import functools

import jax
import jax.numpy as jnp
from jax import lax
from jax.experimental import pallas as pl
from jax.experimental.pallas import tpu as pltpu
from jax.sharding import PartitionSpec as P

F32, BF16 = jnp.float32, jnp.bfloat16
MESH = pl.DeviceIdType.MESH

NZ, NXX = 8, 4


def iota(shape, dim):
    return lax.broadcasted_iota(jnp.int32, shape, dim)


def split_store(w_ref, rows, cols, value):
    high = value.astype(BF16)
    w_ref[0, rows, cols] = high
    w_ref[1, rows, cols] = (value - high.astype(F32)).astype(BF16)


def arrange_taps(taps_ref, pad_ref, out_ref):
    lane, row = iota((8, 128), 1), iota((8, 128), 0)
    used = (lane < 5) | (lane >= 124)
    place = jnp.where(lane < 5, 4 - lane, 132 - lane)
    pad_ref[...] = jnp.zeros_like(pad_ref)
    for fr in range(2):
        for part in range(2):
            pad_ref[2 * fr + part : 2 * fr + part + 1, 0:81] = taps_ref[fr, part : part + 1, :]
    for fr in range(2):
        for part in range(2):
            line = jnp.broadcast_to(pad_ref[2 * fr + part : 2 * fr + part + 1, :], (8, 128))
            for half in range(2):
                index = jnp.where(used, jnp.minimum(9 * (row + 8 * half), 72) + place, 127)
                out_ref[fr, part, 8 * half : 8 * half + 8, :] = jnp.take_along_axis(line, index, axis=1)


def build_weights(d, taps_ref, w_ref, edge_ref):
    row, col = iota((128, 128), 0), iota((128, 128), 1)
    near = jnp.abs(col - row) <= 4
    row8, col8 = iota((8, 128), 0), iota((8, 128), 1)
    low = row8 < 4
    top_mask = col8 - row8 >= 124
    end_mask = col8 - (row8 + 120) <= -124
    edge_ref[72:128, :] = jnp.zeros((56, 256), F32)
    for a in range(9):
        circ = []
        for part in range(2):
            first = jnp.broadcast_to(taps_ref[part, a : a + 1, :], (128, 128))
            circ.append(pltpu.roll(first, 0, 1, stride=1, stride_axis=0))
        d_r, d_i = (jnp.where(near, m, 0.0) for m in circ)
        base = a * 256
        split_store(w_ref, pl.ds(base, 128), pl.ds(0, 128), d_r)
        split_store(w_ref, pl.ds(base, 128), pl.ds(128, 128), d_i)
        split_store(w_ref, pl.ds(base + 128, 128), pl.ds(0, 128), -d_i)
        split_store(w_ref, pl.ds(base + 128, 128), pl.ds(128, 128), d_r)
        t_r, t_i = (jnp.where(top_mask, m[0:8], 0.0) for m in circ)
        e_r, e_i = (jnp.where(end_mask, m[120:128], 0.0) for m in circ)
        rows = pl.ds(a * 8, 8)
        edge_ref[rows, 0:128] = jnp.where(
            d == 0,
            jnp.where(low, t_r, -pltpu.roll(t_i, 4, 0)),
            jnp.where(low, pltpu.roll(e_r, 4, 0), -e_i),
        )
        edge_ref[rows, 128:256] = jnp.where(
            d == 0,
            jnp.where(low, t_i, pltpu.roll(t_r, 4, 0)),
            jnp.where(low, pltpu.roll(e_i, 4, 0), e_r),
        )
    split_store(w_ref, pl.ds(2304, 128), pl.ds(0, 256), edge_ref[...])


def build_lhs(f_ref, l_ref):
    for grp in range(4):

        @pl.loop(0, 8)
        def _(blk):
            row0 = pl.multiple_of(blk * 32, 32)
            out_rows = pl.ds(pl.multiple_of(grp * 256 + blk * 32, 32), 32)
            for a in range(9):
                for part in range(2):
                    l_ref[out_rows, pl.ds(a * 256 + part * 128, 128)] = f_ref[
                        grp, part, pl.ds(row0 + a, 32), :
                    ].astype(BF16)


def build_edge(g_ref, l_ref):
    for grp in range(4):

        @pl.loop(0, 8)
        def _(blk):
            row0 = pl.multiple_of(blk * 32, 32)
            out_rows = pl.ds(pl.multiple_of(grp * 256 + blk * 32, 32), 32)
            edge = g_ref[grp, pl.ds(row0, 32), :]
            for a in range(1, 9):
                edge = edge + pltpu.roll(g_ref[grp, pl.ds(row0 + a, 32), :], 8 * a, 1)
            l_ref[out_rows, pl.ds(2304, 128)] = edge.astype(BF16)


def pack_edge(d, f_ref, out_ref):
    lane = iota((256, 128), 1)
    packed = jnp.zeros((256, 128), F32)
    for grp in range(4):
        for part in range(2):
            first = 8 * grp + 4 * part
            turned = pltpu.roll(f_ref[grp, part, 4:260, :], 4 * (1 - d) + first, 1)
            packed = jnp.where((lane >= first) & (lane < first + 4), turned, packed)
    out_ref[...] = packed.astype(BF16)


def unpack_edge(in_ref, g_ref):
    lane = iota((256, 128), 1)
    packed = in_ref[...].astype(F32)
    for grp in range(4):
        turned = pltpu.roll(packed, 128 - 8 * grp, 1) if grp else packed
        g_ref[grp, 4:260, :] = jnp.where(lane < 8, turned, 0.0)


def top_edge(d, top_ref, g_ref):
    lane = iota((256, 128), 1)
    other = pl.ds(pl.multiple_of((1 - d) * 128, 128), 128)
    for fr in range(2):
        for s in range(2):
            re = pltpu.roll(top_ref[fr, 2 * s, :, other].astype(F32), 4 * d, 1)
            im = pltpu.roll(top_ref[fr, 2 * s + 1, :, other].astype(F32), 4 + 4 * d, 1)
            g_ref[2 * fr + s, 4:260, :] = jnp.where(lane < 4, re, jnp.where(lane < 8, im, 0.0))


def convolve(l_ref, w_ref, o_ref):
    @pl.loop(0, 2)
    def _(m):
        rows = pl.ds(pl.multiple_of(m * 512, 512), 512)
        left = l_ref[rows, :]
        o_ref[rows, :] = jnp.dot(left, w_ref[m, 0], preferred_element_type=F32) + jnp.dot(
            left, w_ref[m, 1], preferred_element_type=F32
        )


def apply_phase(o_ref, screen_ref, weights, f_ref):
    for fr in range(2):

        @pl.loop(0, 16)
        def _(blk):
            row0 = pl.multiple_of(blk * 16, 16)
            angle = (3.0 * weights[fr]) * screen_ref[pl.ds(row0, 16), :]
            cosine, sine = jnp.cos(angle), jnp.sin(angle)
            for s in range(2):
                grp = fr * 2 + s
                rows = pl.ds(pl.multiple_of(grp * 256 + row0, 16), 16)
                re = o_ref[rows, 0:128]
                im = o_ref[rows, 128:256]
                f_ref[grp, 0, pl.ds(row0 + 4, 16), :] = re * cosine - im * sine
                f_ref[grp, 1, pl.ds(row0 + 4, 16), :] = re * sine + im * cosine


def flip_source(f_ref, rev_ref):
    index = 7 - iota((8, 128), 0)
    for fr in range(2):
        for part in range(2):
            for t in range(33):
                rev_ref[fr, part, 8 * (32 - t) : 8 * (32 - t) + 8, :] = jnp.take_along_axis(
                    f_ref[fr * 2, part, 8 * t : 8 * t + 8, :], index, axis=0
                )


def image_piece(f_ref, rev_ref, img_ref, xx):
    @pl.loop(0, NZ)
    def _(z):
        blk = z * NXX + xx
        row0 = pl.multiple_of(blk * 8, 8)
        rev0 = pl.multiple_of(248 - blk * 8, 8)
        for j in range(8):
            s_rows = pl.ds(rev0 + (7 - j), 8)
            r_rows = pl.ds(row0 + j, 8)
            value = jnp.zeros((8, 128), F32)
            for fr in range(2):
                for part in range(2):
                    value = value + rev_ref[fr, part, s_rows, :] * f_ref[fr * 2 + 1, part, r_rows, :]
            to = pl.multiple_of(z * 32 + (j // 4) * 16 + (j % 2) * 8, 8)
            img_ref[(j // 2) % 2, xx, pl.ds(to, 8), :] = value


def kernel(
    total,
    taps_ref, screen_ref, top_ref, out_ref,
    f_ref, g_ref, l_ref, w_ref, edge_ref, o_ref, rev_ref, pad_ref,
    taps_all, screens, edge_tx, edge_rx, img, rx1, tx2, rx2, acc2, tx3, rx3, acc3, rx4,
    local_sem, s0_send, s0_recv, s1_send, s1_recv, s2_send, s2_recv,
    s3_send, s3_recv, s4_send, s4_recv,
):
    d = lax.axis_index("depth")
    f = lax.axis_index("freq")
    core, yhi, xx, z = f % 2, (f // 2) % 2, (f // 4) % NXX, f // 16

    def device(depth=d, zc=z, xc=xx, yc=yhi, cc=core):
        return (depth, ((zc * NXX + xc) * 2 + yc) * 2 + cc)

    x_peers = [device(xc=(xx + off) % NXX) for off in range(1, NXX)]
    z_peers = [device(zc=(z + off) % NZ) for off in range(1, NZ)]
    core_peer = device(cc=1 - core)
    depth_peer = device(depth=1 - d)
    y_peers = [depth_peer, device(yc=1 - yhi), device(depth=1 - d, yc=1 - yhi)]
    everyone = [core_peer] + y_peers + x_peers + z_peers
    barrier = pltpu.get_barrier_semaphore()
    for peer in everyone:
        pl.semaphore_signal(barrier, inc=1, device_id=peer, device_id_type=MESH)

    mine, theirs = (
        pl.ds(pl.multiple_of(half * 128, 128), 128) for half in (d, 1 - d)
    )
    own_screen = pltpu.make_async_copy(screen_ref.at[:, mine], screens.at[d], local_sem.at[0])
    own_screen.start()
    arrange_taps(taps_ref, pad_ref, taps_all.at[d])
    f_ref[:, :, 0:8, :] = jnp.zeros((4, 2, 8, 128), F32)
    f_ref[:, :, 256:264, :] = jnp.zeros((4, 2, 8, 128), F32)
    g_ref[:, 0:8, :] = jnp.zeros((4, 8, 128), F32)
    g_ref[:, 256:264, :] = jnp.zeros((4, 8, 128), F32)
    for fr in range(2):
        for s in range(2):
            for part in range(2):
                f_ref[fr * 2 + s, part, 4:260, :] = top_ref[fr, 2 * s + part, :, mine].astype(F32)
    top_edge(d, top_ref, g_ref)

    pl.semaphore_wait(barrier, len(everyone))

    def remote(src, dst, send, recv, peer):
        return pltpu.make_async_remote_copy(
            src_ref=src, dst_ref=dst, send_sem=send, recv_sem=recv,
            device_id=peer, device_id_type=MESH,
        )

    swap_taps = remote(taps_all.at[d], taps_all.at[d], s0_send.at[0], s0_recv.at[0], depth_peer)
    swap_screen = remote(
        screen_ref.at[:, theirs], screens.at[d], s0_send.at[1], s0_recv.at[1], depth_peer
    )
    swap_edge = remote(edge_tx, edge_rx, s0_send.at[2], s0_recv.at[2], depth_peer)
    swap_taps.start()
    swap_screen.start()
    weights = [(2 * f + fr + 1).astype(F32) / total for fr in range(2)]

    def stage1_copy(k, off):
        xp = (xx + off) % NXX
        return remote(
            img.at[k, 1 - core, xp], rx1.at[k, off], s1_send.at[k, off], s1_recv.at[k, off], core_peer
        )

    def stage2_copy(k, off):
        return remote(
            tx2.at[k, off - 1], rx2.at[k, off - 1],
            s2_send.at[k, off - 1], s2_recv.at[k, off - 1], x_peers[off - 1],
        )

    def stage3_copy(k, off):
        return remote(
            tx3.at[k, off - 1], rx3.at[k, off - 1],
            s3_send.at[k, off - 1], s3_recv.at[k, off - 1], z_peers[off - 1],
        )

    def stage4_keep(k):
        return remote(
            acc3.at[k, 1 - yhi], rx4.at[k, 0], s4_send.at[k, 0], s4_recv.at[k, 0], y_peers[1]
        )

    def stage4_give(k, yc):
        return remote(
            acc3.at[k, yc], rx4.at[k, 1 + yhi], s4_send.at[k, 1 + yc], s4_recv.at[k, 1 + yhi],
            device(depth=k, yc=yc),
        )

    def stage4_get(k, yc):
        return remote(
            acc3.at[k, 0], rx4.at[k, 1 + yc], s4_send.at[k, 0], s4_recv.at[k, 1 + yc], depth_peer
        )

    def make_image(k):
        flip_source(f_ref, rev_ref)
        for off in (1, 2, 3, 0):
            image_piece(f_ref, rev_ref, img.at[k], (xx + off) % NXX)
            stage1_copy(k, off).start()

    def after_core(k):
        for off in (1, 2, 3, 0):
            xp = (xx + off) % NXX
            stage1_copy(k, off).wait_recv()

            @pl.loop(0, 8)
            def _(part):
                rows = pl.ds(pl.multiple_of(part * 32, 32), 32)
                value = img[k, core, xp, rows, :] + rx1[k, off, rows, :]
                if off:
                    tx2[k, off - 1, rows, :] = value.astype(BF16)
                else:
                    acc2[k, part] = value

            if off:
                stage2_copy(k, off).start()

    def after_x(k):
        for off in range(1, NXX):
            stage2_copy(k, off).wait_recv()

        def total_of(part):
            rows = pl.ds(pl.multiple_of(part * 32, 32), 32)
            value = acc2[k, part]
            for off in range(1, NXX):
                value = value + rx2[k, off - 1, rows, :].astype(F32)
            return value

        for off in (4, 3, 5, 2, 6, 1, 7):
            tx3[k, off - 1] = total_of((z + off) % NZ).astype(BF16)
            stage3_copy(k, off).start()
        acc2[k, z] = total_of(z)

    def after_z(k):
        for off in range(1, NZ):
            stage3_copy(k, off).wait_recv()
        value = acc2[k, z]
        for off in range(1, NZ):
            value = value + rx3[k, off - 1].astype(F32)
        acc3[k] = value.reshape(2, 16, 128)

        @pl.when(d == k)
        def _():
            stage4_keep(k).start()

        @pl.when(d != k)
        def _():
            for yc in range(2):
                stage4_give(k, yc).start()

    def after_y(k):
        @pl.when(d == k)
        def _():
            stage4_keep(k).wait_recv()
            for yc in range(2):
                stage4_get(k, yc).wait_recv()
            scale = total ** -0.5
            near_half = (acc3[k, yhi] + rx4[k, 0]) * scale
            far_half = (rx4[k, 1] + rx4[k, 2]) * scale
            for low in range(2):
                rows = slice(low * 8, low * 8 + 8)
                out_ref[:, pl.ds(low * 256 + k * 128, 128)] = near_half[rows]
                out_ref[:, pl.ds(low * 256 + (1 - k) * 128, 128)] = far_half[rows]

    build_lhs(f_ref, l_ref)
    build_edge(g_ref, l_ref)
    swap_taps.wait_recv()
    for fr in range(2):
        build_weights(d, taps_all.at[0, fr], w_ref.at[fr], edge_ref)
    convolve(l_ref, w_ref, o_ref)
    own_screen.wait()
    swap_screen.wait_recv()
    apply_phase(o_ref, screens.at[0], weights, f_ref)
    pack_edge(d, f_ref, edge_tx)
    swap_edge.start()
    make_image(0)
    build_lhs(f_ref, l_ref)
    after_core(0)
    for fr in range(2):
        build_weights(d, taps_all.at[1, fr], w_ref.at[fr], edge_ref)
    swap_edge.wait_recv()
    unpack_edge(edge_rx, g_ref)
    build_edge(g_ref, l_ref)
    convolve(l_ref, w_ref, o_ref)
    apply_phase(o_ref, screens.at[1], weights, f_ref)
    after_x(0)
    make_image(1)
    after_core(1)
    after_z(0)
    after_x(1)
    after_y(0)
    after_z(1)
    after_y(1)

    swap_edge.wait_send()
    swap_taps.wait_send()
    swap_screen.wait_send()
    for k in range(2):
        for off in range(NXX):
            stage1_copy(k, off).wait_send()
        for off in range(1, NXX):
            stage2_copy(k, off).wait_send()
        for off in range(1, NZ):
            stage3_copy(k, off).wait_send()

        @pl.when(d == k)
        def _():
            stage4_keep(k).wait_send()

        @pl.when(d != k)
        def _():
            for yc in range(2):
                stage4_give(k, yc).wait_send()


def migrate(total, taps, screen, top):
    dma = pltpu.SemaphoreType.DMA
    vmem = pl.BlockSpec(memory_space=pltpu.VMEM)
    return pl.pallas_call(
        functools.partial(kernel, total),
        out_shape=jax.ShapeDtypeStruct((8, 512), F32),
        in_specs=[vmem] * 3,
        out_specs=vmem,
        scratch_shapes=[
            pltpu.VMEM((4, 2, 264, 128), F32),
            pltpu.VMEM((4, 264, 128), F32),
            pltpu.VMEM((1024, 2432), BF16),
            pltpu.VMEM((2, 2, 2432, 256), BF16),
            pltpu.VMEM((128, 256), F32),
            pltpu.VMEM((1024, 256), F32),
            pltpu.VMEM((2, 2, 264, 128), F32),
            pltpu.VMEM((8, 128), F32),
            pltpu.VMEM((2, 2, 2, 16, 128), F32),
            pltpu.VMEM((2, 256, 128), F32),
            pltpu.VMEM((256, 128), BF16),
            pltpu.VMEM((256, 128), BF16),
            pltpu.VMEM((2, 2, NXX, 256, 128), F32),
            pltpu.VMEM((2, NXX, 256, 128), F32),
            pltpu.VMEM((2, 3, 256, 128), BF16),
            pltpu.VMEM((2, 3, 256, 128), BF16),
            pltpu.VMEM((2, NZ, 32, 128), F32),
            pltpu.VMEM((2, 7, 32, 128), BF16),
            pltpu.VMEM((2, 7, 32, 128), BF16),
            pltpu.VMEM((2, 2, 16, 128), F32),
            pltpu.VMEM((2, 3, 16, 128), F32),
            dma((1,)), dma((3,)), dma((3,)), dma((2, 4)), dma((2, 4)), dma((2, 3)), dma((2, 3)),
            dma((2, 7)), dma((2, 7)), dma((2, 3)), dma((2, 3)),
        ],
        compiler_params=pltpu.CompilerParams(
            collective_id=0, has_side_effects=True, vmem_limit_bytes=56 * 2**20
        ),
    )(taps, screen, top)


def local(total, top_fields, slowness, kernels, offsets):
    screen = lax.dynamic_slice(slowness[0], (offsets[0, 0], offsets[0, 1]), (256, 256))
    out = migrate(float(total), kernels[0], screen, top_fields[0])
    return out[None, None]


def solution(mesh):
    return jax.shard_map(
        functools.partial(local, 256),
        mesh=mesh,
        in_specs=(
            P(None, "freq", None, None, None),
            P("depth", None, None),
            P("depth", "freq", None, None),
            P(),
        ),
        out_specs=P("depth", None, None, "freq"),
        check_vma=False,
    )
```

time: 71.6 us -> 54.6 us (0.76)
  Pallas kernels: 63 us -> 47 us
  local copies, waits for them, and re-layouts: 4.39 us -> 3.46 us
    pallas_call x1, Pallas kernels: 63 us -> 47 us  [migrate(): pl.pallas_call(functools.partial(kernel, total), out_shape=jax.ShapeDtype...]
    unnamed x7 -> x5, local copies, waits for them, and re-layouts: 1.97 us -> 2.05 us
where the time goes in v2:
time: 54.6 us; the launch traced here: 54.4 us
  Pallas kernels  47 us (86%)
  between operations  3.86 us (7%)
  local copies, waits for them, and re-layouts  3.46 us (6%)
    pallas_call x1, Pallas kernels, migrate(): pl.pallas_call(functools.partial(kernel, total), out_shape=jax.ShapeDtype...  47 us
    unnamed x5, local copies, waits for them, and re-layouts  2.05 us

profile of v2, /device:TPU:8, one launch (start us, length us, event | category | flops | bytes accessed | tf_op | source)
XLA Modules:
  0.0 54.4 jit_solution(869320219755005624)
XLA Ops:
  0.0 0.0 copy-start
  0.0 0.0 copy-start.1
  0.0 0.7 %copy-done.1 = s32[1,2]{1,0:T(1,128)S(1)} copy-done((s32[1,2]{1,0:T(1,128)S(1)}, s32[1,2]{1,0:T(1,128)}, u32[]{:S(2)}) %copy-start.1) | copy-done | bytes 32
  0.7 0.6 %fusion = (s32[1,1]{1,0:T(1,128)}, s32[1,1]{1,0:T(1,128)}) fusion(s32[1,2]{1,0:T(1,128)S(1)} %copy-done.1), kind=kLoop, calls=%fused_computation.1 | loop fusion | bytes 16 | tf_op jit(solution)/shard_map/slice | solution.py:440
  5.1 0.0 copy-done
  5.2 0.8 %dynamic-slice_bitcast_fusion.screen_ref = f32[256,256]{1,0:T(8,128)} fusion(f32[1,384,384]{2,1,0:T(8,128)S(1)} %copy-done, s32[]{:T(128)S(6)} %select_n.6, s32[]{:T(128)S(6)} %select_n.7), kind=kLoop, calls=%fused_computation | loop fusion | bytes 524296 | tf_op jit(solution)/shard_map/dynamic_slice | solution.py:440
  6.0 47.0 %shard_map.46 = f32[8,512]{1,0:T(8,128)} custom-call(f32[2,2,81]{2,1,0:T(2,128)} %bitcast.9, f32[256,256]{1,0:T(8,128)} %dynamic-slice_bitcast_fusion.screen_ref, bf16[2,4,256,256]{3,2,1,0:T(8,128)(2,1)} %bitcast.7), custom_call_target="tpu_custom_call" | custom-call | tf_op jit(solution)/shard_map/pallas_call | solution.py:403
  53.0 1.3 %copy.6 = f32[1,1,8,512]{3,2,1,0:T(8,128)} copy(f32[1,1,8,512]{3,2,1,0:T(8,128)} %bitcast.8) | data formatting | bytes 32768
Async XLA Ops:
  0.0 5.1 %copy-start = (f32[1,384,384]{2,1,0:T(8,128)S(1)}, f32[1,384,384]{2,1,0:T(8,128)}, u32[]{:S(2)}) copy-start(f32[1,384,384]{2,1,0:T(8,128)} %param.5) | copy-start | bytes 1769476
  0.0 0.7 %copy-start.1 = (s32[1,2]{1,0:T(1,128)S(1)}, s32[1,2]{1,0:T(1,128)}, u32[]{:S(2)}) copy-start(s32[1,2]{1,0:T(1,128)} %param.7) | copy-start | bytes 28

commit v3 on v2

--- a/solution.py
+++ b/solution.py
@@ -74,33 +74,6 @@
     split_store(w_ref, pl.ds(2304, 128), pl.ds(0, 256), edge_ref[...])
 
 
-def build_lhs(f_ref, l_ref):
-    for grp in range(4):
-
-        @pl.loop(0, 8)
-        def _(blk):
-            row0 = pl.multiple_of(blk * 32, 32)
-            out_rows = pl.ds(pl.multiple_of(grp * 256 + blk * 32, 32), 32)
-            for a in range(9):
-                for part in range(2):
-                    l_ref[out_rows, pl.ds(a * 256 + part * 128, 128)] = f_ref[
-                        grp, part, pl.ds(row0 + a, 32), :
-                    ].astype(BF16)
-
-
-def build_edge(g_ref, l_ref):
-    for grp in range(4):
-
-        @pl.loop(0, 8)
-        def _(blk):
-            row0 = pl.multiple_of(blk * 32, 32)
-            out_rows = pl.ds(pl.multiple_of(grp * 256 + blk * 32, 32), 32)
-            edge = g_ref[grp, pl.ds(row0, 32), :]
-            for a in range(1, 9):
-                edge = edge + pltpu.roll(g_ref[grp, pl.ds(row0 + a, 32), :], 8 * a, 1)
-            l_ref[out_rows, pl.ds(2304, 128)] = edge.astype(BF16)
-
-
 def pack_edge(d, f_ref, out_ref):
     lane = iota((256, 128), 1)
     packed = jnp.zeros((256, 128), F32)
@@ -130,14 +103,63 @@
             g_ref[2 * fr + s, 4:260, :] = jnp.where(lane < 4, re, jnp.where(lane < 8, im, 0.0))
 
 
-def convolve(l_ref, w_ref, o_ref):
-    @pl.loop(0, 2)
-    def _(m):
-        rows = pl.ds(pl.multiple_of(m * 512, 512), 512)
-        left = l_ref[rows, :]
-        o_ref[rows, :] = jnp.dot(left, w_ref[m, 0], preferred_element_type=F32) + jnp.dot(
-            left, w_ref[m, 1], preferred_element_type=F32
-        )
+def convolve(f_ref, g_ref, w_ref, o_ref):
+    for fr in range(2):
+        fields = []
+        for grp in (2 * fr, 2 * fr + 1):
+            pieces = [
+                f_ref[grp, part, pl.ds(a, 256), :].astype(BF16) for a in range(9) for part in range(2)
+            ]
+            edge = g_ref[grp, pl.ds(0, 256), :]
+            for a in range(1, 9):
+                edge = edge + pltpu.roll(g_ref[grp, pl.ds(a, 256), :], 8 * a, 1)
+            pieces.append(edge.astype(BF16))
+            fields.append(jnp.concatenate(pieces, axis=1))
+        left = jnp.concatenate(fields, axis=0)
+        o_ref[fr * 512 : fr * 512 + 512, :] = jnp.dot(
+            left, w_ref[fr, 0], preferred_element_type=F32
+        ) + jnp.dot(left, w_ref[fr, 1], preferred_element_type=F32)
+
+
+def cos_sin(angle):
+    turns = jnp.round(angle * 0.6366197723675814)
+    y = ((angle - turns * 1.5703125) - turns * 4.837512969970703e-4) - turns * 7.549789948768648e-8
+    z = y * y
+    sine = y + y * z * (-1.6666654611e-1 + z * (8.3321608736e-3 + z * -1.9515295891e-4))
+    cosine = (1.0 - 0.5 * z) + z * z * (
+        4.166664568298827e-2 + z * (-1.388731625493765e-3 + z * 2.443315711809948e-5)
+    )
+    quarter = turns.astype(jnp.int32)
+    odd = (quarter & 1) == 1
+    out_sine = jnp.where(odd, cosine, sine)
+    out_cosine = jnp.where(odd, sine, cosine)
+    return (
+        jnp.where(((quarter + 1) & 2) == 2, -out_cosine, out_cosine),
+        jnp.where((quarter & 2) == 2, -out_sine, out_sine),
+    )
+
+
+def cut_screen(slow_ref, off_x, off_y, half, wide_ref, out_ref):
+    lane = iota((32, 128), 1)
+    start = jnp.zeros((32, 128), jnp.int32) + (off_y + 128 * half)
+
+    @pl.loop(0, 12)
+    def _(blk):
+        rows = pl.ds(pl.multiple_of(blk * 32, 32), 32)
+        value = jnp.where(
+            lane >= start,
+            slow_ref[rows, 0:128],
+            jnp.where(lane + 128 >= start, slow_ref[rows, 128:256], slow_ref[rows, 256:384]),
+        )
+        for bit in range(7):
+            turned = pltpu.roll(value, 128 - (1 << bit), 1)
+            value = jnp.where((start & (1 << bit)) > 0, turned, value)
+        wide_ref[rows, :] = value
+
+    @pl.loop(0, 8)
+    def _(blk):
+        row0 = pl.multiple_of(blk * 32, 32)
+        out_ref[pl.ds(row0, 32), :] = wide_ref[pl.ds(off_x + row0, 32), :]
 
 
 def apply_phase(o_ref, screen_ref, weights, f_ref):
@@ -147,7 +169,7 @@
         def _(blk):
             row0 = pl.multiple_of(blk * 16, 16)
             angle = (3.0 * weights[fr]) * screen_ref[pl.ds(row0, 16), :]
-            cosine, sine = jnp.cos(angle), jnp.sin(angle)
+            cosine, sine = cos_sin(angle)
             for s in range(2):
                 grp = fr * 2 + s
                 rows = pl.ds(pl.multiple_of(grp * 256 + row0, 16), 16)
@@ -186,10 +208,10 @@
 
 def kernel(
     total,
-    taps_ref, screen_ref, top_ref, out_ref,
-    f_ref, g_ref, l_ref, w_ref, edge_ref, o_ref, rev_ref, pad_ref,
-    taps_all, screens, edge_tx, edge_rx, img, rx1, tx2, rx2, acc2, tx3, rx3, acc3, rx4,
-    local_sem, s0_send, s0_recv, s1_send, s1_recv, s2_send, s2_recv,
+    offsets_ref, taps_ref, slow_ref, top_ref, out_ref,
+    f_ref, g_ref, w_ref, edge_ref, o_ref, rev_ref, pad_ref,
+    wide_ref, taps_all, screens, screen_tx, edge_tx, edge_rx, img, rx1, tx2, rx2, acc2, tx3, rx3, acc3, rx4,
+    s0_send, s0_recv, s1_send, s1_recv, s2_send, s2_recv,
     s3_send, s3_recv, s4_send, s4_recv,
 ):
     d = lax.axis_index("depth")
@@ -209,11 +231,7 @@
     for peer in everyone:
         pl.semaphore_signal(barrier, inc=1, device_id=peer, device_id_type=MESH)
 
-    mine, theirs = (
-        pl.ds(pl.multiple_of(half * 128, 128), 128) for half in (d, 1 - d)
-    )
-    own_screen = pltpu.make_async_copy(screen_ref.at[:, mine], screens.at[d], local_sem.at[0])
-    own_screen.start()
+    mine = pl.ds(pl.multiple_of(d * 128, 128), 128)
     arrange_taps(taps_ref, pad_ref, taps_all.at[d])
     f_ref[:, :, 0:8, :] = jnp.zeros((4, 2, 8, 128), F32)
     f_ref[:, :, 256:264, :] = jnp.zeros((4, 2, 8, 128), F32)
@@ -224,6 +242,11 @@
             for part in range(2):
                 f_ref[fr * 2 + s, part, 4:260, :] = top_ref[fr, 2 * s + part, :, mine].astype(F32)
     top_edge(d, top_ref, g_ref)
+    off_x, off_y = offsets_ref[0, 0], offsets_ref[0, 1]
+    cut_screen(slow_ref, off_x, off_y, 1 - d, wide_ref, screen_tx)
+    cut_screen(slow_ref, off_x, off_y, d, wide_ref, screens.at[d])
+    for fr in range(2):
+        build_weights(d, taps_all.at[d, fr], w_ref.at[d, fr], edge_ref)
 
     pl.semaphore_wait(barrier, len(everyone))
 
@@ -235,7 +258,7 @@
 
     swap_taps = remote(taps_all.at[d], taps_all.at[d], s0_send.at[0], s0_recv.at[0], depth_peer)
     swap_screen = remote(
-        screen_ref.at[:, theirs], screens.at[d], s0_send.at[1], s0_recv.at[1], depth_peer
+        screen_tx, screens.at[d], s0_send.at[1], s0_recv.at[1], depth_peer
     )
     swap_edge = remote(edge_tx, edge_rx, s0_send.at[2], s0_recv.at[2], depth_peer)
     swap_taps.start()
@@ -338,37 +361,29 @@
             stage4_keep(k).wait_recv()
             for yc in range(2):
                 stage4_get(k, yc).wait_recv()
-            scale = total ** -0.5
-            near_half = (acc3[k, yhi] + rx4[k, 0]) * scale
-            far_half = (rx4[k, 1] + rx4[k, 2]) * scale
+            near_half = acc3[k, yhi] + rx4[k, 0]
+            far_half = rx4[k, 1] + rx4[k, 2]
             for low in range(2):
                 rows = slice(low * 8, low * 8 + 8)
                 out_ref[:, pl.ds(low * 256 + k * 128, 128)] = near_half[rows]
                 out_ref[:, pl.ds(low * 256 + (1 - k) * 128, 128)] = far_half[rows]
 
-    build_lhs(f_ref, l_ref)
-    build_edge(g_ref, l_ref)
     swap_taps.wait_recv()
     for fr in range(2):
-        build_weights(d, taps_all.at[0, fr], w_ref.at[fr], edge_ref)
-    convolve(l_ref, w_ref, o_ref)
-    own_screen.wait()
+        build_weights(d, taps_all.at[1 - d, fr], w_ref.at[1 - d, fr], edge_ref)
+    convolve(f_ref, g_ref, w_ref.at[0], o_ref)
     swap_screen.wait_recv()
     apply_phase(o_ref, screens.at[0], weights, f_ref)
     pack_edge(d, f_ref, edge_tx)
     swap_edge.start()
     make_image(0)
-    build_lhs(f_ref, l_ref)
-    after_core(0)
-    for fr in range(2):
-        build_weights(d, taps_all.at[1, fr], w_ref.at[fr], edge_ref)
     swap_edge.wait_recv()
     unpack_edge(edge_rx, g_ref)
-    build_edge(g_ref, l_ref)
-    convolve(l_ref, w_ref, o_ref)
+    after_core(0)
+    convolve(f_ref, g_ref, w_ref.at[1], o_ref)
     apply_phase(o_ref, screens.at[1], weights, f_ref)
+    make_image(1)
     after_x(0)
-    make_image(1)
     after_core(1)
     after_z(0)
     after_x(1)
@@ -397,25 +412,26 @@
                 stage4_give(k, yc).wait_send()
 
 
-def migrate(total, taps, screen, top):
+def migrate(total, offsets, taps, slowness, top):
     dma = pltpu.SemaphoreType.DMA
     vmem = pl.BlockSpec(memory_space=pltpu.VMEM)
     return pl.pallas_call(
         functools.partial(kernel, total),
         out_shape=jax.ShapeDtypeStruct((8, 512), F32),
-        in_specs=[vmem] * 3,
+        in_specs=[pl.BlockSpec(memory_space=pltpu.SMEM)] + [vmem] * 3,
         out_specs=vmem,
         scratch_shapes=[
             pltpu.VMEM((4, 2, 264, 128), F32),
             pltpu.VMEM((4, 264, 128), F32),
-            pltpu.VMEM((1024, 2432), BF16),
-            pltpu.VMEM((2, 2, 2432, 256), BF16),
+            pltpu.VMEM((2, 2, 2, 2432, 256), BF16),
             pltpu.VMEM((128, 256), F32),
             pltpu.VMEM((1024, 256), F32),
             pltpu.VMEM((2, 2, 264, 128), F32),
             pltpu.VMEM((8, 128), F32),
+            pltpu.VMEM((384, 128), F32),
             pltpu.VMEM((2, 2, 2, 16, 128), F32),
             pltpu.VMEM((2, 256, 128), F32),
+            pltpu.VMEM((256, 128), F32),
             pltpu.VMEM((256, 128), BF16),
             pltpu.VMEM((256, 128), BF16),
             pltpu.VMEM((2, 2, NXX, 256, 128), F32),
@@ -427,19 +443,18 @@
             pltpu.VMEM((2, 7, 32, 128), BF16),
             pltpu.VMEM((2, 2, 16, 128), F32),
             pltpu.VMEM((2, 3, 16, 128), F32),
-            dma((1,)), dma((3,)), dma((3,)), dma((2, 4)), dma((2, 4)), dma((2, 3)), dma((2, 3)),
+            dma((3,)), dma((3,)), dma((2, 4)), dma((2, 4)), dma((2, 3)), dma((2, 3)),
             dma((2, 7)), dma((2, 7)), dma((2, 3)), dma((2, 3)),
         ],
         compiler_params=pltpu.CompilerParams(
             collective_id=0, has_side_effects=True, vmem_limit_bytes=56 * 2**20
         ),
-    )(taps, screen, top)
+    )(offsets, taps, slowness, top)
 
 
 def local(total, top_fields, slowness, kernels, offsets):
-    screen = lax.dynamic_slice(slowness[0], (offsets[0, 0], offsets[0, 1]), (256, 256))
-    out = migrate(float(total), kernels[0], screen, top_fields[0])
-    return out[None, None]
+    out = migrate(float(total), offsets, kernels[0], slowness[0], top_fields[0])
+    return out[None, None] * float(total) ** -0.5
 
 
 def solution(mesh):

time: 54.6 us -> 53.8 us (0.985)
  Pallas kernels: 47 us -> 52.3 us
  between operations: 3.86 us -> 0.01 us
  local copies, waits for them, and re-layouts: 3.46 us -> 0 us
  other arithmetic: 0 us -> 1.33 us
    pallas_call x1, Pallas kernels: 47 us -> 52.3 us  [migrate(): pl.pallas_call(functools.partial(kernel, total), out_shape=jax.ShapeDtype...]
    unnamed x5 -> x0, local copies, waits for them, and re-layouts: 2.05 us -> none
    mul x0 -> x1, other arithmetic: none -> 1.33 us  [local(): return out[None, None] * float(total) ** (-0.5)]
    dynamic_slice x1 -> x0, local copies, waits for them, and re-layouts: 0.84 us -> none  [local(): lax.dynamic_slice(slowness[0], (offsets[0, 0], offsets[0, 1]), (256, 256))]
    slice x1 -> x0, local copies, waits for them, and re-layouts: 0.58 us -> none  [local(): offsets[0, 1]]
where the time goes in v3:
time: 53.8 us; the launch traced here: 53.6 us
  Pallas kernels  52.3 us (97%)
  other arithmetic  1.33 us (2%)
    pallas_call x1, Pallas kernels, migrate(): pl.pallas_call(functools.partial(kernel, total), out_shape=jax.ShapeDtype...  52.3 us
    mul x1, other arithmetic, local(): return out[None, None] * float(total) ** (-0.5)  1.33 us

profile of v3, /device:TPU:8, one launch (start us, length us, event | category | flops | bytes accessed | tf_op | source)
XLA Modules:
  0.0 53.6 jit_solution(5770406727628800333)
XLA Ops:
  0.0 52.3 %shard_map.46 = f32[8,512]{1,0:T(8,128)} custom-call(s32[1,2]{1,0:T(1,128)} %offsets_ref.1, f32[2,2,81]{2,1,0:T(2,128)} %bitcast.7, f32[384,384]{1,0:T(8,128)} %bitcast.6, bf16[2,4,256,256]{3,2,1,0:T(8,128)(2,1)} %bitcast.5), custom_call_target="tpu_custom_call" | custom-call | tf_op jit(solution)/shard_map/pallas_call | solution.py:418
  52.3 1.3 %multiply_bitcast_fusion = f32[1,1,8,512]{3,2,1,0:T(8,128)} fusion(f32[8,512]{1,0:T(8,128)} %shard_map.46), kind=kLoop, calls=%fused_computation | loop fusion | flops 4096 | bytes 32768 | tf_op jit(solution)/shard_map/mul | solution.py:457

commit v4 on v3

v4 whole, which is shorter than its diff:
```python
import functools

import jax
import jax.numpy as jnp
from jax import lax
from jax.experimental import pallas as pl
from jax.experimental.pallas import tpu as pltpu
from jax.sharding import PartitionSpec as P

F32, BF16 = jnp.float32, jnp.bfloat16
MESH = pl.DeviceIdType.MESH

NZ, NXX = 8, 4
X_ORDER = (2, 1, 3, 0)


def iota(shape, dim):
    return lax.broadcasted_iota(jnp.int32, shape, dim)


def split_store(w_ref, rows, cols, value):
    high = value.astype(BF16)
    w_ref[0, rows, cols] = high
    w_ref[1, rows, cols] = (value - high.astype(F32)).astype(BF16)


def arrange_taps(taps_ref, pad_ref, out_ref):
    lane, row = iota((8, 128), 1), iota((8, 128), 0)
    used = (lane < 5) | (lane >= 124)
    place = jnp.where(lane < 5, 4 - lane, 132 - lane)
    pad_ref[...] = jnp.zeros_like(pad_ref)
    for fr in range(2):
        for part in range(2):
            pad_ref[2 * fr + part : 2 * fr + part + 1, 0:81] = taps_ref[fr, part : part + 1, :]
    for fr in range(2):
        for part in range(2):
            line = jnp.broadcast_to(pad_ref[2 * fr + part : 2 * fr + part + 1, :], (8, 128))
            for half in range(2):
                index = jnp.where(used, jnp.minimum(9 * (row + 8 * half), 72) + place, 127)
                out_ref[fr, part, 8 * half : 8 * half + 8, :] = jnp.take_along_axis(line, index, axis=1)


def build_weights(d, taps_ref, w_ref, edge_ref):
    row, col = iota((128, 128), 0), iota((128, 128), 1)
    near = jnp.abs(col - row) <= 4
    row8, col8 = iota((8, 128), 0), iota((8, 128), 1)
    low = row8 < 4
    top_mask = col8 - row8 >= 124
    end_mask = col8 - (row8 + 120) <= -124
    edge_ref[72:128, :] = jnp.zeros((56, 256), F32)
    for a in range(9):
        circ = []
        for part in range(2):
            first = jnp.broadcast_to(taps_ref[part, a : a + 1, :], (128, 128))
            circ.append(pltpu.roll(first, 0, 1, stride=1, stride_axis=0))
        d_r, d_i = (jnp.where(near, m, 0.0) for m in circ)
        base = a * 256
        split_store(w_ref, pl.ds(base, 128), pl.ds(0, 128), d_r)
        split_store(w_ref, pl.ds(base, 128), pl.ds(128, 128), d_i)
        split_store(w_ref, pl.ds(base + 128, 128), pl.ds(0, 128), -d_i)
        split_store(w_ref, pl.ds(base + 128, 128), pl.ds(128, 128), d_r)
        t_r, t_i = (jnp.where(top_mask, m[0:8], 0.0) for m in circ)
        e_r, e_i = (jnp.where(end_mask, m[120:128], 0.0) for m in circ)
        rows = pl.ds(a * 8, 8)
        edge_ref[rows, 0:128] = jnp.where(
            d == 0,
            jnp.where(low, t_r, -pltpu.roll(t_i, 4, 0)),
            jnp.where(low, pltpu.roll(e_r, 4, 0), -e_i),
        )
        edge_ref[rows, 128:256] = jnp.where(
            d == 0,
            jnp.where(low, t_i, pltpu.roll(t_r, 4, 0)),
            jnp.where(low, pltpu.roll(e_i, 4, 0), e_r),
        )
    split_store(w_ref, pl.ds(2304, 128), pl.ds(0, 256), edge_ref[...])


def pack_edge(d, f_ref, out_ref):
    lane = iota((256, 128), 1)
    packed = jnp.zeros((256, 128), F32)
    for grp in range(4):
        for part in range(2):
            first = 8 * grp + 4 * part
            turned = pltpu.roll(f_ref[grp, part, 4:260, :], 4 * (1 - d) + first, 1)
            packed = jnp.where((lane >= first) & (lane < first + 4), turned, packed)
    out_ref[...] = packed.astype(BF16)


def unpack_edge(in_ref, g_ref):
    lane = iota((256, 128), 1)
    packed = in_ref[...].astype(F32)
    for grp in range(4):
        turned = pltpu.roll(packed, 128 - 8 * grp, 1) if grp else packed
        g_ref[grp, 4:260, :] = jnp.where(lane < 8, turned, 0.0)


def top_edge(d, top_ref, g_ref):
    lane = iota((256, 128), 1)
    other = pl.ds(pl.multiple_of((1 - d) * 128, 128), 128)
    for fr in range(2):
        for s in range(2):
            re = pltpu.roll(top_ref[fr, 2 * s, :, other].astype(F32), 4 * d, 1)
            im = pltpu.roll(top_ref[fr, 2 * s + 1, :, other].astype(F32), 4 + 4 * d, 1)
            g_ref[2 * fr + s, 4:260, :] = jnp.where(lane < 4, re, jnp.where(lane < 8, im, 0.0))


def edge_columns(g_ref, grp):
    edge = g_ref[grp, pl.ds(0, 256), :]
    for a in range(1, 9):
        edge = edge + pltpu.roll(g_ref[grp, pl.ds(a, 256), :], 8 * a, 1)
    return edge.astype(BF16)


def convolve(f_ref, w_ref, o_ref, fr, g_ref=None):
    fields = []
    for grp in (2 * fr, 2 * fr + 1):
        pieces = [
            f_ref[grp, part, pl.ds(a, 256), :].astype(BF16) for a in range(9) for part in range(2)
        ]
        if g_ref is not None:
            pieces.append(edge_columns(g_ref, grp))
        fields.append(jnp.concatenate(pieces, axis=1))
    left = jnp.concatenate(fields, axis=0)
    depth = slice(0, left.shape[1])
    o_ref[fr * 512 : fr * 512 + 512, :] = jnp.dot(
        left, w_ref[fr, 0, depth, :], preferred_element_type=F32
    ) + jnp.dot(left, w_ref[fr, 1, depth, :], preferred_element_type=F32)


def add_edge(g_ref, w_ref, o_ref, fr):
    left = jnp.concatenate([edge_columns(g_ref, 2 * fr), edge_columns(g_ref, 2 * fr + 1)], axis=0)
    depth = slice(2304, 2432)
    o_ref[fr * 512 : fr * 512 + 512, :] += jnp.dot(
        left, w_ref[fr, 0, depth, :], preferred_element_type=F32
    ) + jnp.dot(left, w_ref[fr, 1, depth, :], preferred_element_type=F32)


def cos_sin(angle):
    turns = jnp.round(angle * 0.6366197723675814)
    y = ((angle - turns * 1.5703125) - turns * 4.837512969970703e-4) - turns * 7.549789948768648e-8
    z = y * y
    sine = y + y * z * (-1.6666654611e-1 + z * (8.3321608736e-3 + z * -1.9515295891e-4))
    cosine = (1.0 - 0.5 * z) + z * z * (
        4.166664568298827e-2 + z * (-1.388731625493765e-3 + z * 2.443315711809948e-5)
    )
    quarter = turns.astype(jnp.int32)
    odd = (quarter & 1) == 1
    out_sine = jnp.where(odd, cosine, sine)
    out_cosine = jnp.where(odd, sine, cosine)
    return (
        jnp.where(((quarter + 1) & 2) == 2, -out_cosine, out_cosine),
        jnp.where((quarter & 2) == 2, -out_sine, out_sine),
    )


def cut_screen(slow_ref, off_x, off_y, half, wide_ref, out_ref):
    lane = iota((192, 128), 1)
    start = jnp.zeros((192, 128), jnp.int32) + (off_y + 128 * half)
    for rows in (slice(0, 192), slice(192, 384)):
        value = jnp.where(
            lane >= start,
            slow_ref[rows, 0:128],
            jnp.where(lane + 128 >= start, slow_ref[rows, 128:256], slow_ref[rows, 256:384]),
        )
        for bit in range(7):
            turned = pltpu.roll(value, 128 - (1 << bit), 1)
            value = jnp.where((start & (1 << bit)) > 0, turned, value)
        wide_ref[rows, :] = value

    @pl.loop(0, 8)
    def _(blk):
        row0 = pl.multiple_of(blk * 32, 32)
        out_ref[pl.ds(row0, 32), :] = wide_ref[pl.ds(off_x + row0, 32), :]


def apply_phase(o_ref, screen_ref, weights, f_ref):
    for fr in range(2):

        @pl.loop(0, 16)
        def _(blk):
            row0 = pl.multiple_of(blk * 16, 16)
            angle = (3.0 * weights[fr]) * screen_ref[pl.ds(row0, 16), :]
            cosine, sine = cos_sin(angle)
            for s in range(2):
                grp = fr * 2 + s
                rows = pl.ds(pl.multiple_of(grp * 256 + row0, 16), 16)
                re = o_ref[rows, 0:128]
                im = o_ref[rows, 128:256]
                f_ref[grp, 0, pl.ds(row0 + 4, 16), :] = re * cosine - im * sine
                f_ref[grp, 1, pl.ds(row0 + 4, 16), :] = re * sine + im * cosine


def flip_source(f_ref, rev_ref):
    index = 7 - iota((8, 128), 0)
    for fr in range(2):
        for part in range(2):
            for t in range(33):
                rev_ref[fr, part, 8 * (32 - t) : 8 * (32 - t) + 8, :] = jnp.take_along_axis(
                    f_ref[fr * 2, part, 8 * t : 8 * t + 8, :], index, axis=0
                )


def image_piece(f_ref, rev_ref, img_ref, xx):
    @pl.loop(0, NZ)
    def _(z):
        blk = z * NXX + xx
        row0 = pl.multiple_of(blk * 8, 8)
        rev0 = pl.multiple_of(248 - blk * 8, 8)
        for j in range(8):
            s_rows = pl.ds(rev0 + (7 - j), 8)
            r_rows = pl.ds(row0 + j, 8)
            value = jnp.zeros((8, 128), F32)
            for fr in range(2):
                for part in range(2):
                    value = value + rev_ref[fr, part, s_rows, :] * f_ref[fr * 2 + 1, part, r_rows, :]
            to = pl.multiple_of((j // 4) * 128 + z * 16 + (j % 2) * 8, 8)
            img_ref[(j // 2) % 2, xx, pl.ds(to, 8), :] = value


def kernel(
    total,
    offsets_ref, taps_ref, slow_hbm, top_hbm, out_ref,
    slow_ref, top_ref, f_ref, g_ref, w_ref, edge_ref, o_ref, rev_ref, pad_ref, wide_ref,
    taps_all, screens, screen_tx, edge_tx, edge_rx, img, rx1, tx2, rx2, acc, tx3, rx3,
    local_sem, s0_send, s0_recv, s1_send, s1_recv, s2_send, s2_recv, s3_send, s3_recv,
):
    d = lax.axis_index("depth")
    f = lax.axis_index("freq")
    core, yhi, xx, z = f % 2, (f // 2) % 2, (f // 4) % NXX, f // 16

    load_top = pltpu.make_async_copy(top_hbm, top_ref, local_sem.at[0])
    load_slow = pltpu.make_async_copy(slow_hbm, slow_ref, local_sem.at[1])

    def device(depth=d, zc=z, xc=xx, yc=yhi, cc=core):
        return (depth, ((zc * NXX + xc) * 2 + yc) * 2 + cc)

    xs, ys = [(xx + off) % NXX for off in range(NXX)], [yhi, 1 - yhi]
    z_peers = [device(zc=(z + off) % NZ) for off in range(1, NZ)]
    core_peer = device(cc=1 - core)
    depth_peer = device(depth=1 - d)
    plane = [
        device(depth=(d + rel) % 2, xc=xs[xo], yc=ys[yo])
        for rel in range(2) for xo in range(NXX) for yo in range(2)
    ][1:]
    everyone = [core_peer] + plane + z_peers
    barrier = pltpu.get_barrier_semaphore()
    for peer in everyone:
        pl.semaphore_signal(barrier, inc=1, device_id=peer, device_id_type=MESH)
    load_slow.start()
    load_top.start()

    def remote(src, dst, send, recv, peer):
        return pltpu.make_async_remote_copy(
            src_ref=src, dst_ref=dst, send_sem=send, recv_sem=recv,
            device_id=peer, device_id_type=MESH,
        )

    swap_taps = remote(taps_all.at[d], taps_all.at[d], s0_send.at[0], s0_recv.at[0], depth_peer)
    swap_screen = remote(screen_tx, screens.at[d], s0_send.at[1], s0_recv.at[1], depth_peer)
    swap_edge = remote(edge_tx, edge_rx, s0_send.at[2], s0_recv.at[2], depth_peer)
    weights = [(2 * f + fr + 1).astype(F32) / total for fr in range(2)]

    def stage1_copy(k, off):
        return remote(
            img.at[k, 1 - core, xs[off]], rx1.at[k, off],
            s1_send.at[k, off], s1_recv.at[k, off], core_peer,
        )

    def stage2_copy(k, xo, yo):
        at = ((d + k) % 2) * 8 + xo * 2 + yo
        return remote(
            tx2.at[k, xo * 2 + yo], rx2.at[k, at], s2_send.at[k, xo * 2 + yo], s2_recv.at[k, at],
            device(depth=k, xc=xs[xo], yc=ys[yo]),
        )

    def stage2_get(k, at):
        return remote(rx2.at[k, at], rx2.at[k, at], s2_send.at[k, 0], s2_recv.at[k, at], depth_peer)

    def stage3_copy(k, off):
        return remote(
            tx3.at[k, off - 1], rx3.at[k, off - 1],
            s3_send.at[k, off - 1], s3_recv.at[k, off - 1], z_peers[off - 1],
        )

    def make_image(k):
        flip_source(f_ref, rev_ref)
        for off in X_ORDER:
            image_piece(f_ref, rev_ref, img.at[k], xs[off])
            stage1_copy(k, off).start()

    def after_core(k):
        for off in X_ORDER:
            stage1_copy(k, off).wait_recv()
            for yo in (1, 0):
                rows = pl.ds(pl.multiple_of(ys[yo] * 128, 128), 128)
                value = img[k, core, xs[off], rows, :] + rx1[k, off, rows, :]
                if off == 0 and yo == 0:
                    acc[k] = value
                tx2[k, off * 2 + yo] = value.astype(BF16)
                if off == 0 and yo == 0:

                    @pl.when(d != k)
                    def _():
                        stage2_copy(k, 0, 0).start()
                else:
                    stage2_copy(k, off, yo).start()

    def after_plane(k):
        @pl.when(d == k)
        def _():
            for at in range(1, 16):
                stage2_get(k, at).wait_recv()

            def total_of(part):
                rows = pl.ds(pl.multiple_of(part * 16, 16), 16)
                near = acc[k, rows, :]
                for at in range(1, 8):
                    near = near + rx2[k, at, rows, :].astype(F32)
                far = rx2[k, 8, rows, :].astype(F32)
                for at in range(9, 16):
                    far = far + rx2[k, at, rows, :].astype(F32)
                return jnp.concatenate([near, far], axis=0)

            for off in (4, 3, 5, 2, 6, 1, 7):
                tx3[k, off - 1] = total_of((z + off) % NZ).astype(BF16)
                stage3_copy(k, off).start()
            acc[k, 0:32, :] = total_of(z)

    def after_z(k):
        @pl.when(d == k)
        def _():
            for off in range(1, NZ):
                stage3_copy(k, off).wait_recv()
            value = acc[k, 0:32, :]
            for off in range(1, NZ):
                value = value + rx3[k, off - 1].astype(F32)
            for half in range(2):
                lanes = k * 128 if half == 0 else (1 - k) * 128
                for low in range(2):
                    rows = slice(half * 16 + low * 8, half * 16 + low * 8 + 8)
                    out_ref[:, pl.ds(low * 256 + lanes, 128)] = value[rows]

    arrange_taps(taps_ref, pad_ref, taps_all.at[d])
    pl.semaphore_wait(barrier, len(everyone))
    swap_taps.start()
    f_ref[:, :, 0:8, :] = jnp.zeros((4, 2, 8, 128), F32)
    f_ref[:, :, 256:264, :] = jnp.zeros((4, 2, 8, 128), F32)
    g_ref[:, 0:8, :] = jnp.zeros((4, 8, 128), F32)
    g_ref[:, 256:264, :] = jnp.zeros((4, 8, 128), F32)
    off_x, off_y = offsets_ref[0, 0], offsets_ref[0, 1]
    load_slow.wait()
    cut_screen(slow_ref, off_x, off_y, 1 - d, wide_ref, screen_tx)
    swap_screen.start()
    load_top.wait()
    mine = pl.ds(pl.multiple_of(d * 128, 128), 128)
    for fr in range(2):
        for s in range(2):
            for part in range(2):
                f_ref[fr * 2 + s, part, 4:260, :] = top_ref[fr, 2 * s + part, :, mine].astype(F32)
    top_edge(d, top_ref, g_ref)
    cut_screen(slow_ref, off_x, off_y, d, wide_ref, screens.at[d])

    swap_taps.wait_recv()
    for fr in range(2):
        build_weights(d, taps_all.at[0, fr], w_ref.at[0, fr], edge_ref.at[0])
    for fr in range(2):
        convolve(f_ref, w_ref.at[0], o_ref, fr, g_ref)
        build_weights(d, taps_all.at[1, fr], w_ref.at[1, fr], edge_ref.at[1])
    swap_screen.wait_recv()
    apply_phase(o_ref, screens.at[0], weights, f_ref)
    pack_edge(d, f_ref, edge_tx)
    swap_edge.start()
    make_image(0)
    for fr in range(2):
        convolve(f_ref, w_ref.at[1], o_ref, fr)
    after_core(0)
    swap_edge.wait_recv()
    unpack_edge(edge_rx, g_ref)
    for fr in range(2):
        add_edge(g_ref, w_ref.at[1], o_ref, fr)
    apply_phase(o_ref, screens.at[1], weights, f_ref)
    make_image(1)
    after_core(1)
    after_plane(0)
    after_z(0)
    after_plane(1)
    after_z(1)

    swap_taps.wait_send()
    swap_screen.wait_send()
    swap_edge.wait_send()
    for k in range(2):
        for off in range(NXX):
            stage1_copy(k, off).wait_send()
            for yo in range(2):
                if off or yo:
                    stage2_copy(k, off, yo).wait_send()

        @pl.when(d != k)
        def _():
            stage2_copy(k, 0, 0).wait_send()

        @pl.when(d == k)
        def _():
            for off in range(1, NZ):
                stage3_copy(k, off).wait_send()


def migrate(total, offsets, taps, slowness, top):
    dma = pltpu.SemaphoreType.DMA
    vmem = pl.BlockSpec(memory_space=pltpu.VMEM)
    hbm = pl.BlockSpec(memory_space=pl.ANY)
    return pl.pallas_call(
        functools.partial(kernel, total),
        out_shape=jax.ShapeDtypeStruct((8, 512), F32),
        in_specs=[pl.BlockSpec(memory_space=pltpu.SMEM), vmem, hbm, hbm],
        out_specs=vmem,
        scratch_shapes=[
            pltpu.VMEM((384, 384), F32),
            pltpu.VMEM((2, 4, 256, 256), BF16),
            pltpu.VMEM((4, 2, 264, 128), F32),
            pltpu.VMEM((4, 264, 128), F32),
            pltpu.VMEM((2, 2, 2, 2432, 256), BF16),
            pltpu.VMEM((2, 128, 256), F32),
            pltpu.VMEM((1024, 256), F32),
            pltpu.VMEM((2, 2, 264, 128), F32),
            pltpu.VMEM((8, 128), F32),
            pltpu.VMEM((384, 128), F32),
            pltpu.VMEM((2, 2, 2, 16, 128), F32),
            pltpu.VMEM((2, 256, 128), F32),
            pltpu.VMEM((256, 128), F32),
            pltpu.VMEM((256, 128), BF16),
            pltpu.VMEM((256, 128), BF16),
            pltpu.VMEM((2, 2, NXX, 256, 128), F32),
            pltpu.VMEM((2, NXX, 256, 128), F32),
            pltpu.VMEM((2, 8, 128, 128), BF16),
            pltpu.VMEM((2, 16, 128, 128), BF16),
            pltpu.VMEM((2, 128, 128), F32),
            pltpu.VMEM((2, 7, 32, 128), BF16),
            pltpu.VMEM((2, 7, 32, 128), BF16),
            dma((2,)), dma((3,)), dma((3,)), dma((2, 4)), dma((2, 4)), dma((2, 8)), dma((2, 16)),
            dma((2, 7)), dma((2, 7)),
        ],
        compiler_params=pltpu.CompilerParams(
            collective_id=0, has_side_effects=True, vmem_limit_bytes=56 * 2**20
        ),
    )(offsets, taps, slowness, top)


def local(total, top_fields, slowness, kernels, offsets):
    out = migrate(float(total), offsets, kernels[0], slowness[0], top_fields[0])
    return out[None, None] * float(total) ** -0.5


def solution(mesh):
    return jax.shard_map(
        functools.partial(local, 256),
        mesh=mesh,
        in_specs=(
            P(None, "freq", None, None, None),
            P("depth", None, None),
            P("depth", "freq", None, None),
            P(),
        ),
        out_specs=P("depth", None, None, "freq"),
        check_vma=False,
    )
```

time: 53.8 us -> 39.9 us (0.74)
  the two profiles are of different devices: /device:TPU:8 before, /device:TPU:24 now
where the time goes in v4:
time: 39.9 us; the launch traced here: 39.7 us
  Pallas kernels  38.4 us (96%)
  other arithmetic  1.33 us (3%)
    pallas_call x1, Pallas kernels, migrate(): pl.pallas_call(functools.partial(kernel, total), out_shape=jax.ShapeDtype...  38.4 us
    mul x1, other arithmetic, local(): return out[None, None] * float(total) ** (-0.5)  1.33 us

profile of v4, /device:TPU:24, one launch (start us, length us, event | category | flops | bytes accessed | tf_op | source)
XLA Modules:
  0.0 39.7 jit_solution(1691980037209599039)
XLA Ops:
  0.0 38.4 %shard_map.46 = f32[8,512]{1,0:T(8,128)} custom-call(s32[1,2]{1,0:T(1,128)} %offsets_ref.1, f32[2,2,81]{2,1,0:T(2,128)} %bitcast.7, f32[384,384]{1,0:T(8,128)} %bitcast.6, bf16[2,4,256,256]{3,2,1,0:T(8,128)(2,1)} %bitcast.5), custom_call_target="tpu_custom_call" | custom-call | tf_op jit(solution)/shard_map/pallas_call | solution.py:413
  38.4 1.3 %multiply_bitcast_fusion = f32[1,1,8,512]{3,2,1,0:T(8,128)} fusion(f32[8,512]{1,0:T(8,128)} %shard_map.46), kind=kLoop, calls=%fused_computation | loop fusion | flops 4096 | bytes 32768 | tf_op jit(solution)/shard_map/mul | solution.py:452

commit v5 on v4

--- a/solution.py
+++ b/solution.py
@@ -76,22 +76,29 @@
 
 
 def pack_edge(d, f_ref, out_ref):
-    lane = iota((256, 128), 1)
-    packed = jnp.zeros((256, 128), F32)
-    for grp in range(4):
-        for part in range(2):
-            first = 8 * grp + 4 * part
-            turned = pltpu.roll(f_ref[grp, part, 4:260, :], 4 * (1 - d) + first, 1)
-            packed = jnp.where((lane >= first) & (lane < first + 4), turned, packed)
+    lane = iota((64, 128), 1)
+    packed = jnp.zeros((64, 128), F32)
+    for quarter in range(4):
+        rows = slice(4 + 64 * quarter, 68 + 64 * quarter)
+        for grp in range(4):
+            for part in range(2):
+                first = 32 * quarter + 8 * grp + 4 * part
+                turned = pltpu.roll(f_ref[grp, part, rows, :], 4 * (1 - d) + first, 1)
+                packed = jnp.where((lane >= first) & (lane < first + 4), turned, packed)
     out_ref[...] = packed.astype(BF16)
 
 
-def unpack_edge(in_ref, g_ref):
-    lane = iota((256, 128), 1)
+def unpack_edge(in_ref, wide_ref, turned_ref):
+    lane = iota((64, 128), 1)
     packed = in_ref[...].astype(F32)
-    for grp in range(4):
-        turned = pltpu.roll(packed, 128 - 8 * grp, 1) if grp else packed
-        g_ref[grp, 4:260, :] = jnp.where(lane < 8, turned, 0.0)
+    wide_ref[0:8, :] = jnp.zeros((8, 128), F32)
+    wide_ref[256:264, :] = jnp.zeros((8, 128), F32)
+    for quarter in range(4):
+        turned = pltpu.roll(packed, 128 - 32 * quarter, 1) if quarter else packed
+        wide_ref[4 + 64 * quarter : 68 + 64 * quarter, :] = jnp.where(lane < 32, turned, 0.0)
+    wide = wide_ref[0:264, :]
+    for n in range(12):
+        turned_ref[n] = pltpu.roll(wide, (8 * (n - 3)) % 128, 1) if n != 3 else wide
 
 
 def top_edge(d, top_ref, g_ref):
@@ -127,12 +134,21 @@
     ) + jnp.dot(left, w_ref[fr, 1, depth, :], preferred_element_type=F32)
 
 
-def add_edge(g_ref, w_ref, o_ref, fr):
-    left = jnp.concatenate([edge_columns(g_ref, 2 * fr), edge_columns(g_ref, 2 * fr + 1)], axis=0)
-    depth = slice(2304, 2432)
-    o_ref[fr * 512 : fr * 512 + 512, :] += jnp.dot(
-        left, w_ref[fr, 0, depth, :], preferred_element_type=F32
-    ) + jnp.dot(left, w_ref[fr, 1, depth, :], preferred_element_type=F32)
+def add_edge(turned_ref, w_ref, o_ref):
+    lane = iota((256, 128), 1)
+    for fr in range(2):
+        fields = []
+        for grp in (2 * fr, 2 * fr + 1):
+            edge = jnp.zeros((256, 128), F32)
+            for a in range(9):
+                here = (lane >= 8 * a) & (lane < 8 * a + 8)
+                edge = jnp.where(here, turned_ref[a - grp + 3, pl.ds(a, 256), :], edge)
+            fields.append(edge.astype(BF16))
+        left = jnp.concatenate(fields, axis=0)
+        depth = slice(2304, 2432)
+        o_ref[fr * 512 : fr * 512 + 512, :] += jnp.dot(
+            left, w_ref[fr, 0, depth, :], preferred_element_type=F32
+        ) + jnp.dot(left, w_ref[fr, 1, depth, :], preferred_element_type=F32)
 
 
 def cos_sin(angle):
@@ -153,41 +169,40 @@
     )
 
 
-def cut_screen(slow_ref, off_x, off_y, half, wide_ref, out_ref):
-    lane = iota((192, 128), 1)
-    start = jnp.zeros((192, 128), jnp.int32) + (off_y + 128 * half)
-    for rows in (slice(0, 192), slice(192, 384)):
-        value = jnp.where(
-            lane >= start,
-            slow_ref[rows, 0:128],
-            jnp.where(lane + 128 >= start, slow_ref[rows, 128:256], slow_ref[rows, 256:384]),
-        )
-        for bit in range(7):
-            turned = pltpu.roll(value, 128 - (1 << bit), 1)
-            value = jnp.where((start & (1 << bit)) > 0, turned, value)
-        wide_ref[rows, :] = value
-
-    @pl.loop(0, 8)
-    def _(blk):
-        row0 = pl.multiple_of(blk * 32, 32)
-        out_ref[pl.ds(row0, 32), :] = wide_ref[pl.ds(off_x + row0, 32), :]
+def cut_screen(slow_ref, off_x, off_y, sides, wide_ref, outs):
+    value = slow_ref[...]
+    high = value.astype(BF16)
+    rest = value - high.astype(F32)
+    middle = rest.astype(BF16)
+    low = (rest - middle.astype(F32)).astype(BF16)
+    lane = iota((384, 256), 1)
+    column = jnp.where(lane < 128, lane + 128 * sides[0], lane - 128 + 128 * sides[1]) + off_y
+    pick = jnp.where(iota((384, 256), 0) == column, 1.0, 0.0).astype(BF16)
+    high, middle, low = (
+        jnp.dot(part, pick, preferred_element_type=F32) for part in (high, middle, low)
+    )
+    moved = high + (middle + low)
+    wide_ref[0] = moved[:, 0:128]
+    wide_ref[1] = moved[:, 128:256]
+    for side in range(2):
+        outs[side][...] = wide_ref[side, pl.ds(off_x, 256), :]
 
 
 def apply_phase(o_ref, screen_ref, weights, f_ref):
     for fr in range(2):
 
-        @pl.loop(0, 16)
+        @pl.loop(0, 4)
         def _(blk):
-            row0 = pl.multiple_of(blk * 16, 16)
-            angle = (3.0 * weights[fr]) * screen_ref[pl.ds(row0, 16), :]
+            row0 = pl.multiple_of(blk * 64, 64)
+            angle = (3.0 * weights[fr]) * screen_ref[pl.ds(row0, 64), :]
             cosine, sine = cos_sin(angle)
             for s in range(2):
                 grp = fr * 2 + s
-                rows = pl.ds(pl.multiple_of(grp * 256 + row0, 16), 16)
+                rows = pl.ds(pl.multiple_of(grp * 256 + row0, 64), 64)
                 re = o_ref[rows, 0:128]
                 im = o_ref[rows, 128:256]
-                f_ref[grp, 0, pl.ds(row0 + 4, 16), :] = re * cosine - im * sine
-                f_ref[grp, 1, pl.ds(row0 + 4, 16), :] = re * sine + im * cosine
+                f_ref[grp, 0, pl.ds(row0 + 4, 64), :] = re * cosine - im * sine
+                f_ref[grp, 1, pl.ds(row0 + 4, 64), :] = re * sine + im * cosine
 
 
 def flip_source(f_ref, rev_ref):
@@ -220,8 +235,8 @@
 def kernel(
     total,
     offsets_ref, taps_ref, slow_hbm, top_hbm, out_ref,
-    slow_ref, top_ref, f_ref, g_ref, w_ref, edge_ref, o_ref, rev_ref, pad_ref, wide_ref,
-    taps_all, screens, screen_tx, edge_tx, edge_rx, img, rx1, tx2, rx2, acc, tx3, rx3,
+    slow_ref, top_ref, f_ref, g_ref, w_ref, edge_ref, o_ref, rev_ref, pad_ref, wide_ref, cut_ref,
+    taps_all, screens, screen_tx, turned_ref, edge_tx, edge_rx, img, rx1, tx2, rx2, acc, tx3, rx3, own_part,
     local_sem, s0_send, s0_recv, s1_send, s1_recv, s2_send, s2_recv, s3_send, s3_recv,
 ):
     d = lax.axis_index("depth")
@@ -266,20 +281,28 @@
             s1_send.at[k, off], s1_recv.at[k, off], core_peer,
         )
 
-    def stage2_copy(k, xo, yo):
+    def stage2_copy(k, xo, yo, part):
         at = ((d + k) % 2) * 8 + xo * 2 + yo
+        rows = pl.ds(part * 64, 64)
         return remote(
-            tx2.at[k, xo * 2 + yo], rx2.at[k, at], s2_send.at[k, xo * 2 + yo], s2_recv.at[k, at],
+            tx2.at[k, xo * 2 + yo, rows], rx2.at[k, at, rows],
+            s2_send.at[k, part, xo * 2 + yo], s2_recv.at[k, part, at],
             device(depth=k, xc=xs[xo], yc=ys[yo]),
         )
 
-    def stage2_get(k, at):
-        return remote(rx2.at[k, at], rx2.at[k, at], s2_send.at[k, 0], s2_recv.at[k, at], depth_peer)
-
-    def stage3_copy(k, off):
+    def stage2_get(k, at, part):
+        here = rx2.at[k, at, pl.ds(part * 64, 64)]
+        return remote(here, here, s2_send.at[k, part, 0], s2_recv.at[k, part, at], depth_peer)
+
+    def stage3_copy(k, to):
+        off = (to - z + NZ) % NZ
         return remote(
-            tx3.at[k, off - 1], rx3.at[k, off - 1],
-            s3_send.at[k, off - 1], s3_recv.at[k, off - 1], z_peers[off - 1],
+            tx3.at[k, to], rx3.at[k, off], s3_send.at[k, to], s3_recv.at[k, off], device(zc=to)
+        )
+
+    def stage3_get(k, off):
+        return remote(
+            rx3.at[k, off], rx3.at[k, off], s3_send.at[k, 0], s3_recv.at[k, off], depth_peer
         )
 
     def make_image(k):
@@ -297,43 +320,51 @@
                 if off == 0 and yo == 0:
                     acc[k] = value
                 tx2[k, off * 2 + yo] = value.astype(BF16)
-                if off == 0 and yo == 0:
-
-                    @pl.when(d != k)
-                    def _():
-                        stage2_copy(k, 0, 0).start()
-                else:
-                    stage2_copy(k, off, yo).start()
+                if off or yo:
+                    stage2_copy(k, off, yo, 0).start()
+        for off in X_ORDER:
+            for yo in (1, 0):
+                if off or yo:
+                    stage2_copy(k, off, yo, 1).start()
+
+        @pl.when(d != k)
+        def _():
+            for part in range(2):
+                stage2_copy(k, 0, 0, part).start()
 
     def after_plane(k):
         @pl.when(d == k)
         def _():
-            for at in range(1, 16):
-                stage2_get(k, at).wait_recv()
-
-            def total_of(part):
-                rows = pl.ds(pl.multiple_of(part * 16, 16), 16)
-                near = acc[k, rows, :]
-                for at in range(1, 8):
-                    near = near + rx2[k, at, rows, :].astype(F32)
-                far = rx2[k, 8, rows, :].astype(F32)
-                for at in range(9, 16):
-                    far = far + rx2[k, at, rows, :].astype(F32)
-                return jnp.concatenate([near, far], axis=0)
-
-            for off in (4, 3, 5, 2, 6, 1, 7):
-                tx3[k, off - 1] = total_of((z + off) % NZ).astype(BF16)
-                stage3_copy(k, off).start()
-            acc[k, 0:32, :] = total_of(z)
+            for part in range(2):
+                for at in range(1, 16):
+                    stage2_get(k, at, part).wait_recv()
+                for to in range(4 * part, 4 * part + 4):
+                    rows = pl.ds(to * 16, 16)
+                    near = acc[k, rows, :]
+                    for at in range(1, 8):
+                        near = near + rx2[k, at, rows, :].astype(F32)
+                    far = rx2[k, 8, rows, :].astype(F32)
+                    for at in range(9, 16):
+                        far = far + rx2[k, at, rows, :].astype(F32)
+                    value = jnp.concatenate([near, far], axis=0)
+                    tx3[k, to] = value.astype(BF16)
+
+                    @pl.when(z != to)
+                    def _():
+                        stage3_copy(k, to).start()
+
+                    @pl.when(z == to)
+                    def _():
+                        own_part[k] = value
 
     def after_z(k):
         @pl.when(d == k)
         def _():
             for off in range(1, NZ):
-                stage3_copy(k, off).wait_recv()
-            value = acc[k, 0:32, :]
+                stage3_get(k, off).wait_recv()
+            value = own_part[k]
             for off in range(1, NZ):
-                value = value + rx3[k, off - 1].astype(F32)
+                value = value + rx3[k, off].astype(F32)
             for half in range(2):
                 lanes = k * 128 if half == 0 else (1 - k) * 128
                 for low in range(2):
@@ -349,7 +380,7 @@
     g_ref[:, 256:264, :] = jnp.zeros((4, 8, 128), F32)
     off_x, off_y = offsets_ref[0, 0], offsets_ref[0, 1]
     load_slow.wait()
-    cut_screen(slow_ref, off_x, off_y, 1 - d, wide_ref, screen_tx)
+    cut_screen(slow_ref, off_x, off_y, (1 - d, d), cut_ref, (screen_tx, screens.at[d]))
     swap_screen.start()
     load_top.wait()
     mine = pl.ds(pl.multiple_of(d * 128, 128), 128)
@@ -358,7 +389,6 @@
             for part in range(2):
                 f_ref[fr * 2 + s, part, 4:260, :] = top_ref[fr, 2 * s + part, :, mine].astype(F32)
     top_edge(d, top_ref, g_ref)
-    cut_screen(slow_ref, off_x, off_y, d, wide_ref, screens.at[d])
 
     swap_taps.wait_recv()
     for fr in range(2):
@@ -375,9 +405,8 @@
         convolve(f_ref, w_ref.at[1], o_ref, fr)
     after_core(0)
     swap_edge.wait_recv()
-    unpack_edge(edge_rx, g_ref)
-    for fr in range(2):
-        add_edge(g_ref, w_ref.at[1], o_ref, fr)
+    unpack_edge(edge_rx, wide_ref, turned_ref)
+    add_edge(turned_ref, w_ref.at[1], o_ref)
     apply_phase(o_ref, screens.at[1], weights, f_ref)
     make_image(1)
     after_core(1)
@@ -394,16 +423,21 @@
             stage1_copy(k, off).wait_send()
             for yo in range(2):
                 if off or yo:
-                    stage2_copy(k, off, yo).wait_send()
+                    for part in range(2):
+                        stage2_copy(k, off, yo, part).wait_send()
 
         @pl.when(d != k)
         def _():
-            stage2_copy(k, 0, 0).wait_send()
+            for part in range(2):
+                stage2_copy(k, 0, 0, part).wait_send()
 
         @pl.when(d == k)
         def _():
-            for off in range(1, NZ):
-                stage3_copy(k, off).wait_send()
+            for to in range(NZ):
+
+                @pl.when(z != to)
+                def _():
+                    stage3_copy(k, to).wait_send()
 
 
 def migrate(total, offsets, taps, slowness, top):
@@ -412,7 +446,7 @@
     hbm = pl.BlockSpec(memory_space=pl.ANY)
     return pl.pallas_call(
         functools.partial(kernel, total),
-        out_shape=jax.ShapeDtypeStruct((8, 512), F32),
+        out_shape=pltpu.VMEM((8, 512), F32),
         in_specs=[pl.BlockSpec(memory_space=pltpu.SMEM), vmem, hbm, hbm],
         out_specs=vmem,
         scratch_shapes=[
@@ -426,20 +460,23 @@
             pltpu.VMEM((2, 2, 264, 128), F32),
             pltpu.VMEM((8, 128), F32),
             pltpu.VMEM((384, 128), F32),
+            pltpu.VMEM((2, 384, 128), F32),
             pltpu.VMEM((2, 2, 2, 16, 128), F32),
             pltpu.VMEM((2, 256, 128), F32),
             pltpu.VMEM((256, 128), F32),
-            pltpu.VMEM((256, 128), BF16),
-            pltpu.VMEM((256, 128), BF16),
+            pltpu.VMEM((12, 264, 128), F32),
+            pltpu.VMEM((64, 128), BF16),
+            pltpu.VMEM((64, 128), BF16),
             pltpu.VMEM((2, 2, NXX, 256, 128), F32),
             pltpu.VMEM((2, NXX, 256, 128), F32),
             pltpu.VMEM((2, 8, 128, 128), BF16),
             pltpu.VMEM((2, 16, 128, 128), BF16),
             pltpu.VMEM((2, 128, 128), F32),
-            pltpu.VMEM((2, 7, 32, 128), BF16),
-            pltpu.VMEM((2, 7, 32, 128), BF16),
-            dma((2,)), dma((3,)), dma((3,)), dma((2, 4)), dma((2, 4)), dma((2, 8)), dma((2, 16)),
-            dma((2, 7)), dma((2, 7)),
+            pltpu.VMEM((2, 8, 32, 128), BF16),
+            pltpu.VMEM((2, 8, 32, 128), BF16),
+            pltpu.VMEM((2, 32, 128), F32),
+            dma((2,)), dma((3,)), dma((3,)), dma((2, 4)), dma((2, 4)), dma((2, 2, 8)), dma((2, 2, 16)),
+            dma((2, 8)), dma((2, 8)),
         ],
         compiler_params=pltpu.CompilerParams(
             collective_id=0, has_side_effects=True, vmem_limit_bytes=56 * 2**20

time: 39.9 us -> 36.9 us (0.925)
  the two profiles are of different devices: /device:TPU:24 before, /device:TPU:25 now
where the time goes in v5:
time: 36.9 us; the launch traced here: 36.8 us
  Pallas kernels  36.2 us (98%)
  other arithmetic  0.61 us (2%)
    pallas_call x1, Pallas kernels, migrate(): pl.pallas_call(functools.partial(kernel, total), out_shape=pltpu.VMEM((8,...  36.2 us

profile of v5, /device:TPU:25, one launch (start us, length us, event | category | flops | bytes accessed | tf_op | source)
XLA Modules:
  0.0 36.8 jit_solution(6902092013949722760)
XLA Ops:
  0.0 36.2 %shard_map.46 = f32[8,512]{1,0:T(8,128)S(1)} custom-call(s32[1,2]{1,0:T(1,128)} %offsets_ref.1, f32[2,2,81]{2,1,0:T(2,128)} %bitcast.7, f32[384,384]{1,0:T(8,128)} %bitcast.6, bf16[2,4,256,256]{3,2,1,0:T(8,128)(2,1)} %bitcast.5), custom_call_target="tpu_custom_call" | custom-call | tf_op jit(solution)/shard_map/pallas_call | solution.py:447
  36.2 0.6 %multiply_bitcast_fusion = f32[1,1,8,512]{3,2,1,0:T(8,128)} fusion(f32[8,512]{1,0:T(8,128)S(1)} %shard_map.46), kind=kLoop, calls=%fused_computation | loop fusion | flops 4096 | bytes 32768 | tf_op jit(solution)/shard_map/mul | solution.py:489

commit v6 on v5

--- a/solution.py
+++ b/solution.py
@@ -12,6 +12,8 @@
 
 NZ, NXX = 8, 4
 X_ORDER = (2, 1, 3, 0)
+ALL, UPPER, LOWER = (0, 256), (0, 144), (144, 112)
+PARTS = (((0, 2),), ((0, 1), (1, 1)))
 
 
 def iota(shape, dim):
@@ -111,44 +113,52 @@
             g_ref[2 * fr + s, 4:260, :] = jnp.where(lane < 4, re, jnp.where(lane < 8, im, 0.0))
 
 
-def edge_columns(g_ref, grp):
-    edge = g_ref[grp, pl.ds(0, 256), :]
+def edge_columns(g_ref, grp, rows):
+    edge = g_ref[grp, pl.ds(rows[0], rows[1]), :]
     for a in range(1, 9):
-        edge = edge + pltpu.roll(g_ref[grp, pl.ds(a, 256), :], 8 * a, 1)
+        edge = edge + pltpu.roll(g_ref[grp, pl.ds(rows[0] + a, rows[1]), :], 8 * a, 1)
     return edge.astype(BF16)
 
 
-def convolve(f_ref, w_ref, o_ref, fr, g_ref=None):
+def convolve(f_ref, w_ref, o_ref, fr, rows, g_ref=None):
     fields = []
     for grp in (2 * fr, 2 * fr + 1):
         pieces = [
-            f_ref[grp, part, pl.ds(a, 256), :].astype(BF16) for a in range(9) for part in range(2)
+            f_ref[grp, part, pl.ds(rows[0] + a, rows[1]), :].astype(BF16)
+            for a in range(9)
+            for part in range(2)
         ]
         if g_ref is not None:
-            pieces.append(edge_columns(g_ref, grp))
+            pieces.append(edge_columns(g_ref, grp, rows))
         fields.append(jnp.concatenate(pieces, axis=1))
     left = jnp.concatenate(fields, axis=0)
     depth = slice(0, left.shape[1])
-    o_ref[fr * 512 : fr * 512 + 512, :] = jnp.dot(
-        left, w_ref[fr, 0, depth, :], preferred_element_type=F32
-    ) + jnp.dot(left, w_ref[fr, 1, depth, :], preferred_element_type=F32)
-
-
-def add_edge(turned_ref, w_ref, o_ref):
-    lane = iota((256, 128), 1)
+    value = jnp.dot(left, w_ref[fr, 0, depth, :], preferred_element_type=F32) + jnp.dot(
+        left, w_ref[fr, 1, depth, :], preferred_element_type=F32
+    )
+    for s in range(2):
+        first = fr * 512 + s * 256 + rows[0]
+        o_ref[first : first + rows[1], :] = value[s * rows[1] : (s + 1) * rows[1]]
+
+
+def add_edge(turned_ref, w_ref, o_ref, rows):
+    lane = iota((rows[1], 128), 1)
     for fr in range(2):
         fields = []
         for grp in (2 * fr, 2 * fr + 1):
-            edge = jnp.zeros((256, 128), F32)
+            edge = jnp.zeros((rows[1], 128), F32)
             for a in range(9):
                 here = (lane >= 8 * a) & (lane < 8 * a + 8)
-                edge = jnp.where(here, turned_ref[a - grp + 3, pl.ds(a, 256), :], edge)
+                edge = jnp.where(here, turned_ref[a - grp + 3, pl.ds(rows[0] + a, rows[1]), :], edge)
             fields.append(edge.astype(BF16))
         left = jnp.concatenate(fields, axis=0)
         depth = slice(2304, 2432)
-        o_ref[fr * 512 : fr * 512 + 512, :] += jnp.dot(
-            left, w_ref[fr, 0, depth, :], preferred_element_type=F32
-        ) + jnp.dot(left, w_ref[fr, 1, depth, :], preferred_element_type=F32)
+        value = jnp.dot(left, w_ref[fr, 0, depth, :], preferred_element_type=F32) + jnp.dot(
+            left, w_ref[fr, 1, depth, :], preferred_element_type=F32
+        )
+        for s in range(2):
+            first = fr * 512 + s * 256 + rows[0]
+            o_ref[first : first + rows[1], :] += value[s * rows[1] : (s + 1) * rows[1]]
 
 
 def cos_sin(angle):
@@ -188,37 +198,37 @@
         outs[side][...] = wide_ref[side, pl.ds(off_x, 256), :]
 
 
-def apply_phase(o_ref, screen_ref, weights, f_ref):
-    for fr in range(2):
-
-        @pl.loop(0, 4)
+def apply_phase(o_ref, screen_ref, weights, f_ref, rows, size):
+    for fr in range(2):
+
+        @pl.loop(0, rows[1] // size)
         def _(blk):
-            row0 = pl.multiple_of(blk * 64, 64)
-            angle = (3.0 * weights[fr]) * screen_ref[pl.ds(row0, 64), :]
+            row0 = pl.multiple_of(rows[0] + blk * size, 8)
+            angle = (3.0 * weights[fr]) * screen_ref[pl.ds(row0, size), :]
             cosine, sine = cos_sin(angle)
             for s in range(2):
                 grp = fr * 2 + s
-                rows = pl.ds(pl.multiple_of(grp * 256 + row0, 64), 64)
-                re = o_ref[rows, 0:128]
-                im = o_ref[rows, 128:256]
-                f_ref[grp, 0, pl.ds(row0 + 4, 64), :] = re * cosine - im * sine
-                f_ref[grp, 1, pl.ds(row0 + 4, 64), :] = re * sine + im * cosine
-
-
-def flip_source(f_ref, rev_ref):
+                here = pl.ds(pl.multiple_of(grp * 256 + row0, 8), size)
+                re = o_ref[here, 0:128]
+                im = o_ref[here, 128:256]
+                f_ref[grp, 0, pl.ds(row0 + 4, size), :] = re * cosine - im * sine
+                f_ref[grp, 1, pl.ds(row0 + 4, size), :] = re * sine + im * cosine
+
+
+def flip_source(f_ref, rev_ref, tiles):
     index = 7 - iota((8, 128), 0)
     for fr in range(2):
         for part in range(2):
-            for t in range(33):
+            for t in tiles:
                 rev_ref[fr, part, 8 * (32 - t) : 8 * (32 - t) + 8, :] = jnp.take_along_axis(
                     f_ref[fr * 2, part, 8 * t : 8 * t + 8, :], index, axis=0
                 )
 
 
-def image_piece(f_ref, rev_ref, img_ref, xx):
-    @pl.loop(0, NZ)
+def image_piece(f_ref, rev_ref, img_ref, xx, half):
+    @pl.loop(0, NZ // 2)
     def _(z):
-        blk = z * NXX + xx
+        blk = (z + half * 4) * NXX + xx
         row0 = pl.multiple_of(blk * 8, 8)
         rev0 = pl.multiple_of(248 - blk * 8, 8)
         for j in range(8):
@@ -228,14 +238,14 @@
             for fr in range(2):
                 for part in range(2):
                     value = value + rev_ref[fr, part, s_rows, :] * f_ref[fr * 2 + 1, part, r_rows, :]
-            to = pl.multiple_of((j // 4) * 128 + z * 16 + (j % 2) * 8, 8)
+            to = pl.multiple_of(half * 128 + (j // 4) * 64 + z * 16 + (j % 2) * 8, 8)
             img_ref[(j // 2) % 2, xx, pl.ds(to, 8), :] = value
 
 
 def kernel(
     total,
     offsets_ref, taps_ref, slow_hbm, top_hbm, out_ref,
-    slow_ref, top_ref, f_ref, g_ref, w_ref, edge_ref, o_ref, rev_ref, pad_ref, wide_ref, cut_ref,
+    slow_ref, top_ref, f_ref, last_ref, g_ref, w_ref, edge_ref, o_ref, rev_ref, pad_ref, wide_ref, cut_ref,
     taps_all, screens, screen_tx, turned_ref, edge_tx, edge_rx, img, rx1, tx2, rx2, acc, tx3, rx3, own_part,
     local_sem, s0_send, s0_recv, s1_send, s1_recv, s2_send, s2_recv, s3_send, s3_recv,
 ):
@@ -275,93 +285,89 @@
     swap_edge = remote(edge_tx, edge_rx, s0_send.at[2], s0_recv.at[2], depth_peer)
     weights = [(2 * f + fr + 1).astype(F32) / total for fr in range(2)]
 
-    def stage1_copy(k, off):
+    def stage1_copy(k, off, part):
+        rows = pl.ds(part[0] * 128, part[1] * 128)
         return remote(
-            img.at[k, 1 - core, xs[off]], rx1.at[k, off],
-            s1_send.at[k, off], s1_recv.at[k, off], core_peer,
+            img.at[k, 1 - core, xs[off], rows], rx1.at[k, off, rows],
+            s1_send.at[k, part[0], off], s1_recv.at[k, part[0], off], core_peer,
         )
 
     def stage2_copy(k, xo, yo, part):
         at = ((d + k) % 2) * 8 + xo * 2 + yo
-        rows = pl.ds(part * 64, 64)
+        rows = pl.ds(part[0] * 64, part[1] * 64)
         return remote(
             tx2.at[k, xo * 2 + yo, rows], rx2.at[k, at, rows],
-            s2_send.at[k, part, xo * 2 + yo], s2_recv.at[k, part, at],
+            s2_send.at[k, part[0], xo * 2 + yo], s2_recv.at[k, part[0]],
             device(depth=k, xc=xs[xo], yc=ys[yo]),
         )
 
-    def stage2_get(k, at, part):
-        here = rx2.at[k, at, pl.ds(part * 64, 64)]
-        return remote(here, here, s2_send.at[k, part, 0], s2_recv.at[k, part, at], depth_peer)
+    def stage2_get(k, part):
+        here = rx2.at[k, pl.ds(1, 15), pl.ds(part[0] * 64, part[1] * 64)]
+        return remote(here, here, s2_send.at[k, part[0], 0], s2_recv.at[k, part[0]], depth_peer)
 
     def stage3_copy(k, to):
         off = (to - z + NZ) % NZ
         return remote(
-            tx3.at[k, to], rx3.at[k, off], s3_send.at[k, to], s3_recv.at[k, off], device(zc=to)
-        )
-
-    def stage3_get(k, off):
-        return remote(
-            rx3.at[k, off], rx3.at[k, off], s3_send.at[k, 0], s3_recv.at[k, off], depth_peer
-        )
-
-    def make_image(k):
-        flip_source(f_ref, rev_ref)
+            tx3.at[k, to], rx3.at[k, off], s3_send.at[k, to], s3_recv.at[k], device(zc=to)
+        )
+
+    def stage3_get(k):
+        here = rx3.at[k, pl.ds(1, 7)]
+        return remote(here, here, s3_send.at[k, 0], s3_recv.at[k], depth_peer)
+
+    def make_image(k, fields, part):
+        halves = range(part[0], part[0] + part[1])
+        for half in halves:
+            flip_source(fields, rev_ref, (range(17), range(17, 33))[half])
         for off in X_ORDER:
-            image_piece(f_ref, rev_ref, img.at[k], xs[off])
-            stage1_copy(k, off).start()
-
-    def after_core(k):
+            for half in halves:
+                image_piece(fields, rev_ref, img.at[k], xs[off], half)
+            stage1_copy(k, off, part).start()
+
+    def after_core(k, part):
         for off in X_ORDER:
-            stage1_copy(k, off).wait_recv()
+            stage1_copy(k, off, part).wait_recv()
             for yo in (1, 0):
-                rows = pl.ds(pl.multiple_of(ys[yo] * 128, 128), 128)
-                value = img[k, core, xs[off], rows, :] + rx1[k, off, rows, :]
-                if off == 0 and yo == 0:
-                    acc[k] = value
-                tx2[k, off * 2 + yo] = value.astype(BF16)
+                for half in range(part[0], part[0] + part[1]):
+                    rows = pl.ds(pl.multiple_of(half * 128 + ys[yo] * 64, 64), 64)
+                    value = img[k, core, xs[off], rows, :] + rx1[k, off, rows, :]
+                    if off == 0 and yo == 0:
+                        acc[k, half * 64 : half * 64 + 64, :] = value
+                    tx2[k, off * 2 + yo, half * 64 : half * 64 + 64, :] = value.astype(BF16)
                 if off or yo:
-                    stage2_copy(k, off, yo, 0).start()
-        for off in X_ORDER:
-            for yo in (1, 0):
-                if off or yo:
-                    stage2_copy(k, off, yo, 1).start()
+                    stage2_copy(k, off, yo, part).start()
 
         @pl.when(d != k)
         def _():
-            for part in range(2):
-                stage2_copy(k, 0, 0, part).start()
-
-    def after_plane(k):
+            stage2_copy(k, 0, 0, part).start()
+
+    def after_plane(k, part):
         @pl.when(d == k)
         def _():
-            for part in range(2):
-                for at in range(1, 16):
-                    stage2_get(k, at, part).wait_recv()
-                for to in range(4 * part, 4 * part + 4):
-                    rows = pl.ds(to * 16, 16)
-                    near = acc[k, rows, :]
-                    for at in range(1, 8):
-                        near = near + rx2[k, at, rows, :].astype(F32)
-                    far = rx2[k, 8, rows, :].astype(F32)
-                    for at in range(9, 16):
-                        far = far + rx2[k, at, rows, :].astype(F32)
-                    value = jnp.concatenate([near, far], axis=0)
-                    tx3[k, to] = value.astype(BF16)
-
-                    @pl.when(z != to)
-                    def _():
-                        stage3_copy(k, to).start()
-
-                    @pl.when(z == to)
-                    def _():
-                        own_part[k] = value
+            stage2_get(k, part).wait_recv()
+            for to in range(4 * part[0], 4 * part[0] + 4 * part[1]):
+                rows = pl.ds(to * 16, 16)
+                near = acc[k, rows, :]
+                for at in range(1, 8):
+                    near = near + rx2[k, at, rows, :].astype(F32)
+                far = rx2[k, 8, rows, :].astype(F32)
+                for at in range(9, 16):
+                    far = far + rx2[k, at, rows, :].astype(F32)
+                value = jnp.concatenate([near, far], axis=0)
+                tx3[k, to] = value.astype(BF16)
+
+                @pl.when(z != to)
+                def _():
+                    stage3_copy(k, to).start()
+
+                @pl.when(z == to)
+                def _():
+                    own_part[k] = value
 
     def after_z(k):
         @pl.when(d == k)
         def _():
-            for off in range(1, NZ):
-                stage3_get(k, off).wait_recv()
+            stage3_get(k).wait_recv()
             value = own_part[k]
             for off in range(1, NZ):
                 value = value + rx3[k, off].astype(F32)
@@ -374,8 +380,9 @@
     arrange_taps(taps_ref, pad_ref, taps_all.at[d])
     pl.semaphore_wait(barrier, len(everyone))
     swap_taps.start()
-    f_ref[:, :, 0:8, :] = jnp.zeros((4, 2, 8, 128), F32)
-    f_ref[:, :, 256:264, :] = jnp.zeros((4, 2, 8, 128), F32)
+    for ref in (f_ref, last_ref):
+        ref[:, :, 0:8, :] = jnp.zeros((4, 2, 8, 128), F32)
+        ref[:, :, 256:264, :] = jnp.zeros((4, 2, 8, 128), F32)
     g_ref[:, 0:8, :] = jnp.zeros((4, 8, 128), F32)
     g_ref[:, 256:264, :] = jnp.zeros((4, 8, 128), F32)
     off_x, off_y = offsets_ref[0, 0], offsets_ref[0, 1]
@@ -394,50 +401,63 @@
     for fr in range(2):
         build_weights(d, taps_all.at[0, fr], w_ref.at[0, fr], edge_ref.at[0])
     for fr in range(2):
-        convolve(f_ref, w_ref.at[0], o_ref, fr, g_ref)
+        convolve(f_ref, w_ref.at[0], o_ref, fr, ALL, g_ref)
         build_weights(d, taps_all.at[1, fr], w_ref.at[1, fr], edge_ref.at[1])
     swap_screen.wait_recv()
-    apply_phase(o_ref, screens.at[0], weights, f_ref)
+    apply_phase(o_ref, screens.at[0], weights, f_ref, ALL, 64)
     pack_edge(d, f_ref, edge_tx)
     swap_edge.start()
-    make_image(0)
-    for fr in range(2):
-        convolve(f_ref, w_ref.at[1], o_ref, fr)
-    after_core(0)
+    make_image(0, f_ref, PARTS[0][0])
+    for fr in range(2):
+        convolve(f_ref, w_ref.at[1], o_ref, fr, UPPER)
+    after_core(0, PARTS[0][0])
     swap_edge.wait_recv()
     unpack_edge(edge_rx, wide_ref, turned_ref)
-    add_edge(turned_ref, w_ref.at[1], o_ref)
-    apply_phase(o_ref, screens.at[1], weights, f_ref)
-    make_image(1)
-    after_core(1)
-    after_plane(0)
-    after_z(0)
-    after_plane(1)
-    after_z(1)
-
+    add_edge(turned_ref, w_ref.at[1], o_ref, UPPER)
+    apply_phase(o_ref, screens.at[1], weights, last_ref, UPPER, 48)
+    make_image(1, last_ref, PARTS[1][0])
+    for fr in range(2):
+        convolve(f_ref, w_ref.at[1], o_ref, fr, LOWER)
+    add_edge(turned_ref, w_ref.at[1], o_ref, LOWER)
+    apply_phase(o_ref, screens.at[1], weights, last_ref, LOWER, 56)
+    make_image(1, last_ref, PARTS[1][1])
+    after_core(1, PARTS[1][0])
+    after_core(1, PARTS[1][1])
+    def sent(k):
+        for part in PARTS[k]:
+            for off in range(NXX):
+                stage1_copy(k, off, part).wait_send()
+                for yo in range(2):
+                    if off or yo:
+                        stage2_copy(k, off, yo, part).wait_send()
+
+        @pl.when(d != k)
+        def _():
+            for part in PARTS[k]:
+                stage2_copy(k, 0, 0, part).wait_send()
+
+    def z_sent(k):
+        @pl.when(d == k)
+        def _():
+            for to in range(NZ):
+
+                @pl.when(z != to)
+                def _():
+                    stage3_copy(k, to).wait_send()
+
+    for part in PARTS[0]:
+        after_plane(0, part)
+    sent(0)
     swap_taps.wait_send()
     swap_screen.wait_send()
     swap_edge.wait_send()
-    for k in range(2):
-        for off in range(NXX):
-            stage1_copy(k, off).wait_send()
-            for yo in range(2):
-                if off or yo:
-                    for part in range(2):
-                        stage2_copy(k, off, yo, part).wait_send()
-
-        @pl.when(d != k)
-        def _():
-            for part in range(2):
-                stage2_copy(k, 0, 0, part).wait_send()
-
-        @pl.when(d == k)
-        def _():
-            for to in range(NZ):
-
-                @pl.when(z != to)
-                def _():
-                    stage3_copy(k, to).wait_send()
+    after_z(0)
+    for part in PARTS[1]:
+        after_plane(1, part)
+    sent(1)
+    z_sent(0)
+    after_z(1)
+    z_sent(1)
 
 
 def migrate(total, offsets, taps, slowness, top):
@@ -452,6 +472,7 @@
         scratch_shapes=[
             pltpu.VMEM((384, 384), F32),
             pltpu.VMEM((2, 4, 256, 256), BF16),
+            pltpu.VMEM((4, 2, 264, 128), F32),
             pltpu.VMEM((4, 2, 264, 128), F32),
             pltpu.VMEM((4, 264, 128), F32),
             pltpu.VMEM((2, 2, 2, 2432, 256), BF16),
@@ -475,8 +496,8 @@
             pltpu.VMEM((2, 8, 32, 128), BF16),
             pltpu.VMEM((2, 8, 32, 128), BF16),
             pltpu.VMEM((2, 32, 128), F32),
-            dma((2,)), dma((3,)), dma((3,)), dma((2, 4)), dma((2, 4)), dma((2, 2, 8)), dma((2, 2, 16)),
-            dma((2, 8)), dma((2, 8)),
+            dma((2,)), dma((3,)), dma((3,)), dma((2, 2, 4)), dma((2, 2, 4)), dma((2, 2, 8)), dma((2, 2)),
+            dma((2, 8)), dma((2,)),
         ],
         compiler_params=pltpu.CompilerParams(
             collective_id=0, has_side_effects=True, vmem_limit_bytes=56 * 2**20

time: 36.9 us -> 36.2 us (0.981)
  the two profiles are of different devices: /device:TPU:25 before, /device:TPU:8 now
where the time goes in v6:
time: 36.2 us; the launch traced here: 36.1 us
  Pallas kernels  35.5 us (98%)
  other arithmetic  0.61 us (2%)
    pallas_call x1, Pallas kernels, migrate(): pl.pallas_call(functools.partial(kernel, total), out_shape=pltpu.VMEM((8,...  35.5 us

profile of v6, /device:TPU:8, one launch (start us, length us, event | category | flops | bytes accessed | tf_op | source)
XLA Modules:
  0.0 36.1 jit_solution(16134257448725317393)
XLA Ops:
  0.0 35.5 %shard_map.46 = f32[8,512]{1,0:T(8,128)S(1)} custom-call(s32[1,2]{1,0:T(1,128)} %offsets_ref.1, f32[2,2,81]{2,1,0:T(2,128)} %bitcast.7, f32[384,384]{1,0:T(8,128)} %bitcast.6, bf16[2,4,256,256]{3,2,1,0:T(8,128)(2,1)} %bitcast.5), custom_call_target="tpu_custom_call" | custom-call | tf_op jit(solution)/shard_map/pallas_call | solution.py:467
  35.5 0.6 %multiply_bitcast_fusion = f32[1,1,8,512]{3,2,1,0:T(8,128)} fusion(f32[8,512]{1,0:T(8,128)S(1)} %shard_map.46), kind=kLoop, calls=%fused_computation | loop fusion | flops 4096 | bytes 32768 | tf_op jit(solution)/shard_map/mul | solution.py:510

commit v7 on v6

--- a/solution.py
+++ b/solution.py
@@ -345,8 +345,10 @@
         @pl.when(d == k)
         def _():
             stage2_get(k, part).wait_recv()
-            for to in range(4 * part[0], 4 * part[0] + 4 * part[1]):
-                rows = pl.ds(to * 16, 16)
+            count = 4 * part[1]
+            for step in range(count):
+                to = 4 * part[0] + (z + step) % count
+                rows = pl.ds(pl.multiple_of(to * 16, 16), 16)
                 near = acc[k, rows, :]
                 for at in range(1, 8):
                     near = near + rx2[k, at, rows, :].astype(F32)
@@ -375,7 +377,7 @@
                 lanes = k * 128 if half == 0 else (1 - k) * 128
                 for low in range(2):
                     rows = slice(half * 16 + low * 8, half * 16 + low * 8 + 8)
-                    out_ref[:, pl.ds(low * 256 + lanes, 128)] = value[rows]
+                    out_ref[:, pl.ds(low * 256 + lanes, 128)] = value[rows] * total**-0.5
 
     arrange_taps(taps_ref, pad_ref, taps_all.at[d])
     pl.semaphore_wait(barrier, len(everyone))
@@ -507,7 +509,7 @@
 
 def local(total, top_fields, slowness, kernels, offsets):
     out = migrate(float(total), offsets, kernels[0], slowness[0], top_fields[0])
-    return out[None, None] * float(total) ** -0.5
+    return out[None, None]
 
 
 def solution(mesh):

time: 36.2 us -> 36.2 us (level)
  other arithmetic: 0.61 us -> 0 us
  local copies, waits for them, and re-layouts: 0 us -> 0.61 us
    mul x1 -> x0, other arithmetic: 0.61 us -> none  [local(): return out[None, None] * float(total) ** (-0.5)]
    unnamed x0 -> x1, local copies, waits for them, and re-layouts: none -> 0.61 us
where the time goes in v7:
time: 36.2 us; the launch traced here: 36.1 us
  Pallas kernels  35.5 us (98%)
  local copies, waits for them, and re-layouts  0.61 us (2%)
    pallas_call x1, Pallas kernels, migrate(): pl.pallas_call(functools.partial(kernel, total), out_shape=pltpu.VMEM((8,...  35.5 us

profile of v7, /device:TPU:8, one launch (start us, length us, event | category | flops | bytes accessed | tf_op | source)
XLA Modules:
  0.0 36.1 jit_solution(8164151135042121842)
XLA Ops:
  0.0 35.5 %shard_map.46 = f32[8,512]{1,0:T(8,128)S(1)} custom-call(s32[1,2]{1,0:T(1,128)} %offsets_ref.1, f32[2,2,81]{2,1,0:T(2,128)} %bitcast.7, f32[384,384]{1,0:T(8,128)} %bitcast.6, bf16[2,4,256,256]{3,2,1,0:T(8,128)(2,1)} %bitcast.5), custom_call_target="tpu_custom_call" | custom-call | tf_op jit(solution)/shard_map/pallas_call | solution.py:469
  35.5 0.6 %copy.6 = f32[1,1,8,512]{3,2,1,0:T(8,128)} copy(f32[1,1,8,512]{3,2,1,0:T(8,128)S(1)} %bitcast.4) | data formatting | bytes 32768
